TPU v7x, 128 devices: a whole 4x4x4 slice. The times are simulated.
128 devices in a mesh: chain: 8 (over y, z_hi), resp: 16 (over x, z_lo, core).
Axes of the slice: x: 4, y: 4, z: 4 (z_hi: 2, z_lo: 2; z = z_hi * 2 + z_lo), core: 2. Of those that a mesh axis runs over, the one named last changes fastest.
Arguments:
- q_prompt: bfloat16 [4096, 8192], P('chain', 'resp'), may hold values from -8 to 8
- k_prompt: bfloat16 [4096, 1024], P(('chain', 'resp')), may hold values from -8 to 8
- v_prompt: bfloat16 [4096, 1024], P(('chain', 'resp')), may hold values from -6 to 6
- q_resp: bfloat16 [16, 512, 8192], P('resp', None, 'chain'), may hold values from -8 to 8
- k_resp: bfloat16 [16, 512, 1024], P('resp', None, 'chain'), may hold values from -6 to 6
- v_resp: bfloat16 [16, 512, 1024], P('resp', None, 'chain'), may hold values from -6 to 6
- tree_table: int32 [16, 8], P('resp'), may hold values from -1 to 6, as said below
- lengths: int32 [16], P('resp'), may hold values from 256 to 512, as said below
Outputs:
- prompt_out: bfloat16 [4096, 8192], P('chain', 'resp')
- resp_out: bfloat16 [16, 512, 8192], P('resp', None, 'chain')
Inputs may be any that keep to these rules, and one draw needn't show every extreme that they name: `tree_table`: entry j of a response's row is -1 (the block has no parent) or the index of an earlier block of that response; entry 0 is -1. `lengths`: some response has 512 live tokens.
All inputs are finite; a program needn't handle non-finite values.
Results may differ from a plain program's by a relative error of at most 0.009.
Values may be sent and summed in bfloat16 or wider, within the bound.
No kernel may reach another device: no remote copies, remote signals or barrier semaphores. Data moves between devices by JAX's collectives and lax.ppermute only.
A program may use at most 64 MiB of HBM per device.

v0:
```python
import jax
import jax.numpy as jnp
from jax import lax
from jax.sharding import PartitionSpec as P

QH = 64
KVH = 8
HD = 128
RBLK = 8


def from_behind(block, axis, distance):
    devices = range(lax.axis_size(axis))
    route = [(i - distance, i) for i in devices if i - distance in devices]
    return lax.ppermute(block, axis, route)


def tree_visible(parent, live_len, row_count, blocks):
    span_rows = row_count // blocks
    block_ids = jnp.arange(blocks, dtype=jnp.int32)
    parent_hot = (parent[:, None] == block_ids[None, :]).astype(jnp.float32)
    ancestry = jnp.eye(blocks, dtype=jnp.float32)
    for which_block in range(blocks):
        upward = jnp.dot(parent_hot[which_block], ancestry, precision=lax.Precision.HIGHEST)
        ancestry = ancestry.at[which_block].set(ancestry[which_block] + upward)
    wide = jnp.repeat(jnp.repeat(ancestry, span_rows, 0), span_rows, 1) > 0.5
    places = jnp.arange(row_count, dtype=jnp.int32)
    return wide & (places[None, :] <= places[:, None]) & (places[None, :] < live_len)


def fresh_state(kv_heads, group_size, row_count, head_dim):
    run_max = jnp.full((kv_heads, group_size, row_count), -1e30, jnp.float32)
    run_sum = jnp.zeros((kv_heads, group_size, row_count), jnp.float32)
    run_acc = jnp.zeros((kv_heads, group_size, row_count, head_dim), jnp.float32)
    return (run_max, run_sum, run_acc)


def attend_block(carried, queries, key_rows, value_rows, visible, factor):
    run_max, run_sum, run_acc = carried
    scores = (
        jnp.einsum("pkgd,skd->kgps", queries, key_rows, preferred_element_type=jnp.float32) * factor
    )
    if visible is None:
        capped = scores
    else:
        capped = jnp.where(visible, scores, -1e30)
    new_max = jnp.maximum(run_max, jnp.max(capped, axis=-1))
    weights = jnp.exp(scores - new_max[..., None])
    if visible is not None:
        weights = jnp.where(visible, weights, 0.0)
    rescale = jnp.exp(run_max - new_max)
    run_sum = run_sum * rescale + jnp.sum(weights, axis=-1)
    added = jnp.einsum(
        "kgps,skd->kgpd",
        weights.astype(jnp.bfloat16),
        value_rows,
        preferred_element_type=jnp.float32,
    )
    run_acc = run_acc * rescale[..., None] + added
    return (new_max, run_sum, run_acc)


def absorb_keys(carried, queries, key_rows, value_rows, factor):
    key_count = key_rows.shape[0]
    span_rows = 512
    blocks = key_count // span_rows
    stacked = (
        key_rows.reshape((blocks, span_rows) + key_rows.shape[1:]),
        value_rows.reshape((blocks, span_rows) + value_rows.shape[1:]),
    )

    def one_block(running, pieces):
        return (attend_block(running, queries, pieces[0], pieces[1], None, factor), None)

    carried, unused = lax.scan(one_block, carried, stacked)
    return carried


def finish(carried):
    run_max, run_sum, run_acc = carried
    return run_acc / run_sum[..., None]


def on_device(q_prompt, k_prompt, v_prompt, q_resp, k_resp, v_resp, tree_table, lengths):
    factor = HD ** (-0.5)
    group_size = QH // KVH
    chain_count = lax.axis_size("chain")
    stretch_rows = q_prompt.shape[0]
    sub_rows = k_prompt.shape[0]
    heads_here = q_prompt.shape[1] // HD
    kv_here = max(1, heads_here // group_size)
    whole_k, whole_v = (
        lax.all_gather(k_prompt, "resp", axis=0, tiled=True),
        lax.all_gather(v_prompt, "resp", axis=0, tiled=True),
    )
    first_col = lax.axis_index("resp") * heads_here // group_size * HD
    stretch_k = lax.dynamic_slice_in_dim(whole_k, first_col, kv_here * HD, 1)
    stretch_v = lax.dynamic_slice_in_dim(whole_v, first_col, kv_here * HD, 1)
    queries = q_prompt.reshape(stretch_rows, kv_here, heads_here // kv_here, HD)
    carried = fresh_state(kv_here, heads_here // kv_here, stretch_rows, HD)
    positions = jnp.arange(stretch_rows, dtype=jnp.int32)
    causal = positions[:, None] >= positions[None, :]
    carried = attend_block(
        carried,
        queries,
        stretch_k.reshape(stretch_rows, kv_here, HD),
        stretch_v.reshape(stretch_rows, kv_here, HD),
        causal,
        factor,
    )
    paired = jnp.stack([stretch_k, stretch_v])
    chain_pos = lax.axis_index("chain")
    moving = paired
    for hop_index in range(1, chain_count):
        moving = from_behind(moving, "chain", 1)
        carried = attend_block(
            carried,
            queries,
            moving[0].reshape(stretch_rows, kv_here, HD),
            moving[1].reshape(stretch_rows, kv_here, HD),
            chain_pos >= hop_index,
            factor,
        )
    prompt_out = (
        finish(carried)
        .transpose(2, 0, 1, 3)
        .reshape(stretch_rows, heads_here * HD)
        .astype(jnp.bfloat16)
    )
    resp_rows = q_resp.shape[1]
    kv_resp = k_resp.shape[2] // HD
    resp_queries = q_resp[0].reshape(resp_rows, kv_resp, group_size, HD)
    own_keys = k_resp[0].reshape(resp_rows, kv_resp, HD)
    own_values = v_resp[0].reshape(resp_rows, kv_resp, HD)
    live_len = lengths[0]
    visible = tree_visible(tree_table[0], live_len, resp_rows, RBLK)
    answer = fresh_state(kv_resp, group_size, resp_rows, HD)
    answer = attend_block(answer, resp_queries, own_keys, own_values, visible, factor)
    head_k = k_prompt.reshape(sub_rows, chain_count, kv_resp * HD)
    head_v = v_prompt.reshape(sub_rows, chain_count, kv_resp * HD)
    sent_k, sent_v = (
        lax.all_to_all(head_k, "chain", split_axis=1, concat_axis=0, tiled=True),
        lax.all_to_all(head_v, "chain", split_axis=1, concat_axis=0, tiled=True),
    )
    answer = absorb_keys(
        answer,
        resp_queries,
        lax.all_gather(sent_k, "resp", axis=0, tiled=True),
        lax.all_gather(sent_v, "resp", axis=0, tiled=True),
        factor,
    )
    joined = finish(answer).transpose(2, 0, 1, 3).reshape(resp_rows, kv_resp * group_size * HD)
    live_rows = jnp.arange(resp_rows, dtype=jnp.int32) < live_len
    resp_out = jnp.where(live_rows[:, None], joined, 0.0).astype(jnp.bfloat16)[None]
    return (prompt_out, resp_out)


def solution(mesh):
    placed = (
        P("chain", "resp"),
        P(("chain", "resp"), None),
        P(("chain", "resp"), None),
        P("resp", None, "chain"),
        P("resp", None, "chain"),
        P("resp", None, "chain"),
        P("resp", None),
        P("resp"),
    )
    return jax.shard_map(
        on_device,
        mesh=mesh,
        in_specs=placed,
        out_specs=(P("chain", "resp"), P("resp", None, "chain")),
        check_vma=False,
    )
```

profile of v0, /device:TPU:8, one launch (start us, length us, event | category | flops | bytes accessed | tf_op | source)
XLA Modules:
  0.0 304.4 jit_solution(4586167996599065212)
XLA Ops:
  8.7 1.5 copy_bitcast_fusion.1
  10.1 8.2 %all-to-all-start = ((bf16[32,8,128]{2,0,1:T(8,128)(2,1)}), bf16[32,8,128]{2,0,1:T(8,128)(2,1)S(1)}, u32[]{:S(2)}, u32[]{:S(2)}) async-start(bf16[32,8,128]{2,0,1:T(8,128)(2,1)} %copy_bitcast_fusion.1), calls=%async_computation | async-start | bytes 131072 | tf_op jit(solution)/shard_map/all_to_all | solution.py:142
  18.4 1.5 copy_bitcast_fusion
  19.9 4.8 %all-to-all-done = bf16[32,8,128]{2,0,1:T(8,128)(2,1)S(1)} async-done(((bf16[32,8,128]{2,0,1:T(8,128)(2,1)}), bf16[32,8,128]{2,0,1:T(8,128)(2,1)S(1)}, u32[]{:S(2)}, u32[]{:S(2)}) %all-to-all-start) | async-done | bytes 65568 | tf_op jit(solution)/shard_map/all_to_all | solution.py:142
  24.7 4.7 %all-to-all-start.1 = ((bf16[32,8,128]{2,0,1:T(8,128)(2,1)}), bf16[32,8,128]{2,0,1:T(8,128)(2,1)S(1)}, u32[]{:S(2)}, u32[]{:S(2)}) async-start(bf16[32,8,128]{2,0,1:T(8,128)(2,1)} %copy_bitcast_fusion), calls=%async_computation.1 | async-start | bytes 131072 | tf_op jit(solution)/shard_map/all_to_all | solution.py:143
  33.1 1.5 copy.173
  34.8 5.7 %fusion.20 = (f32[8,512]{1,0:T(8,128)S(1)}, f32[512,512,8]{1,0,2:T(8,128)}) fusion(pred[512,512]{0,1:T(8,128)(4,1)S(1)} %fusion.167, bf16[512,8,128]{2,1,0:T(8,128)(2,1)S(1)} %bitcast.658, bf16[1,512,128]{2,1,0:T(8,128)(2,1)} %param.30), kind=kOutput, calls=%fused_computation.25 | convolution fusion | flops 543158272 | bytes 9846784 | tf_op jit(solution)/shard_map/pkgd,skd->kgps/dot_general | solution.py:41
  41.2 5.2 %fusion.24 = f32[8,512]{1,0:T(8,128)S(1)} fusion(f32[512,512,8]{1,0,2:T(8,128)} %get-tuple-element.222, f32[8,512]{1,0:T(8,128)S(1)} %get-tuple-element.202, pred[512,512]{0,1:T(8,128)(4,1)S(1)} %fusion.167), kind=kLoop, calls=%fused_computation.29 | loop fusion | flops 8384512 | bytes 8683520 | tf_op jit(solution)/shard_map/reduce_sum | solution.py:52
  47.0 1.3 copy.142
  48.4 4.8 %add_bitcast_fusion = f32[1,8,512,128]{3,2,1,0:T(8,128)S(1)} fusion(f32[512,512,8]{1,0,2:T(8,128)} %get-tuple-element.222, f32[8,512]{1,0:T(8,128)S(1)} %get-tuple-element.202, pred[512,512]{0,1:T(8,128)(4,1)S(1)} %fusion.167, f32[8,512]{1,0:T(8,128)S(1)} %get-tuple-element.200, bf16[1,512,128]{2,1,0:T(8,128)(2,1)S(1)} %copy-done.7), kind=kOutput, calls=%fused_computation.99 | convolution fusion | flops 545783808 | bytes 10911744 | tf_op jit(solution)/shard_map/kgps,skd->kgpd/dot_general | solution.py:53
  54.1 24.7 %all-gather.5.cloned.1.call-done = bf16[512,1024]{1,0:T(8,128)(2,1)} async-done(((bf16[32,1024]{1,0:T(8,128)(2,1)}), bf16[512,1024]{1,0:T(8,128)(2,1)}) %all-gather.5.cloned.1.call-update) | async-done | bytes 1048592 | tf_op jit(solution)/shard_map/all_gather | solution.py:93
  79.8 4.9 %collective-permute-start = (bf16[2,512,128]{2,1,0:T(8,128)(2,1)S(1)}, bf16[2,512,128]{2,1,0:T(8,128)(2,1)}, u32[]{:S(2)}, u32[]{:S(2)}) collective-permute-start(bf16[2,512,128]{2,1,0:T(8,128)(2,1)S(1)} %pad_maximum_fusion), channel_id=1, source_target_pairs={{0,16},{16,32},{32,48},{48,64},{64,80},{80,96},{96,112},{1,17},{17... | collective-permute-start | bytes 786440 | tf_op jit(solution)/shard_map/ppermute | solution.py:15
  84.8 3.7 %fusion.47 = (f32[4,512]{1,0:T(4,128)S(1)}, f32[512,512,4]{1,0,2:T(8,128)}) fusion(pred[512,512]{0,1:T(8,128)(4,1)S(1)} %iota_compare_fusion.1, bf16[512,1024]{1,0:T(8,128)(2,1)} %all-gather.5.cloned.1.call-done, s32[]{:T(128)S(6)} %select_n.107, bf16[512,512]{1,0:T(8,128)(2,1)S(1)} %copy-done), kind=kOutput, calls=%fused_computation.68 | convolution fusion | flops 271579136 | bytes 5120004 | tf_op jit(solution)/shard_map/pkgd,skd->kgps/dot_general | solution.py:41
  88.5 25.2 %all-gather.9.cloned.1.call-done = bf16[4096,1,128]{2,0,1:T(8,128)(2,1)} async-done(((bf16[256,1,128]{2,0,1:T(8,128)(2,1)}), bf16[4096,1,128]{2,0,1:T(8,128)(2,1)}) %all-gather.9.cloned.1.call-update) | async-done | bytes 1048592 | tf_op jit(solution)/shard_map/all_gather | solution.py:148
  113.7 34.1 %all-gather.11.cloned.1.call-done = bf16[4096,1,128]{2,0,1:T(8,128)(2,1)} async-done(((bf16[256,1,128]{2,0,1:T(8,128)(2,1)}), bf16[4096,1,128]{2,0,1:T(8,128)(2,1)}) %all-gather.11.cloned.1.call-update) | async-done | bytes 1048592 | tf_op jit(solution)/shard_map/all_gather | solution.py:149
  147.8 58.9 %while.22 = (s32[]{:T(128)}, f32[1,8,512]{2,1,0:T(8,128)S(1)}, f32[1,8,512]{2,1,0:T(8,128)S(1)}, f32[1,8,512,128]{3,2,1,0:T(8,128)S(1)}, bf16[8,512,1,128]{3,1,2...) while((s32[]{:T(128)}, f32[1,8,512]{2,1,0:T(8,128)S(1)}, ...), condition=%wide.region_21.22_spmd, body=%wide.region_18.21_spmd.sunk | while | flops 1091579904 | bytes 30933092 | solution.py:75
  147.8 2.6 bitcast_reduce_fusion.2
  150.4 1.4 fusion.263
  151.8 3.3 %bitcast_add_fusion.6 = f32[1,8,512,128]{3,2,1,0:T(8,128)S(1)} fusion(f32[1,8,512,128]{3,2,1,0:T(8,128)S(1)} %get-tuple-element.295, f32[512,512,8]{1,0,2:T(8,128)S(1)} %get-tuple-element.282, f32[8,512]{1,0:T(8,128)S(1)} %bitcast.657, f32[8,512]{1,0:T(8,128)S(1)} %get-tuple-element.283, bf16[8,512,1,128]{3,1,2,0:T(8,128)(2,1)} %get-tuple-element.306, ...), kind=kOutput, calls=%fused_computation.9.clone.1 | convolution fusion | flops 544210944 | bytes 12746756 | tf_op jit(solution)/shard_map/while/body/eval_jaxpr/kgps,skd->kgpd/dot_general | solution.py:53
  155.1 2.6 bitcast_reduce_fusion.2
  157.7 1.4 fusion.263
  159.2 3.3 %bitcast_add_fusion.6 = f32[1,8,512,128]{3,2,1,0:T(8,128)S(1)} fusion(f32[1,8,512,128]{3,2,1,0:T(8,128)S(1)} %get-tuple-element.295, f32[512,512,8]{1,0,2:T(8,128)S(1)} %get-tuple-element.282, f32[8,512]{1,0:T(8,128)S(1)} %bitcast.657, f32[8,512]{1,0:T(8,128)S(1)} %get-tuple-element.283, bf16[8,512,1,128]{3,1,2,0:T(8,128)(2,1)} %get-tuple-element.306, ...), kind=kOutput, calls=%fused_computation.9.clone.1 | convolution fusion | flops 544210944 | bytes 12746756 | tf_op jit(solution)/shard_map/while/body/eval_jaxpr/kgps,skd->kgpd/dot_general | solution.py:53
  162.5 2.6 bitcast_reduce_fusion.2
  165.1 1.4 fusion.263
  166.5 3.3 %bitcast_add_fusion.6 = f32[1,8,512,128]{3,2,1,0:T(8,128)S(1)} fusion(f32[1,8,512,128]{3,2,1,0:T(8,128)S(1)} %get-tuple-element.295, f32[512,512,8]{1,0,2:T(8,128)S(1)} %get-tuple-element.282, f32[8,512]{1,0:T(8,128)S(1)} %bitcast.657, f32[8,512]{1,0:T(8,128)S(1)} %get-tuple-element.283, bf16[8,512,1,128]{3,1,2,0:T(8,128)(2,1)} %get-tuple-element.306, ...), kind=kOutput, calls=%fused_computation.9.clone.1 | convolution fusion | flops 544210944 | bytes 12746756 | tf_op jit(solution)/shard_map/while/body/eval_jaxpr/kgps,skd->kgpd/dot_general | solution.py:53
  169.9 2.6 bitcast_reduce_fusion.2
  172.5 1.4 fusion.263
  173.9 3.3 %bitcast_add_fusion.6 = f32[1,8,512,128]{3,2,1,0:T(8,128)S(1)} fusion(f32[1,8,512,128]{3,2,1,0:T(8,128)S(1)} %get-tuple-element.295, f32[512,512,8]{1,0,2:T(8,128)S(1)} %get-tuple-element.282, f32[8,512]{1,0:T(8,128)S(1)} %bitcast.657, f32[8,512]{1,0:T(8,128)S(1)} %get-tuple-element.283, bf16[8,512,1,128]{3,1,2,0:T(8,128)(2,1)} %get-tuple-element.306, ...), kind=kOutput, calls=%fused_computation.9.clone.1 | convolution fusion | flops 544210944 | bytes 12746756 | tf_op jit(solution)/shard_map/while/body/eval_jaxpr/kgps,skd->kgpd/dot_general | solution.py:53
  177.2 2.6 bitcast_reduce_fusion.2
  179.8 1.4 fusion.263
  181.2 3.3 %bitcast_add_fusion.6 = f32[1,8,512,128]{3,2,1,0:T(8,128)S(1)} fusion(f32[1,8,512,128]{3,2,1,0:T(8,128)S(1)} %get-tuple-element.295, f32[512,512,8]{1,0,2:T(8,128)S(1)} %get-tuple-element.282, f32[8,512]{1,0:T(8,128)S(1)} %bitcast.657, f32[8,512]{1,0:T(8,128)S(1)} %get-tuple-element.283, bf16[8,512,1,128]{3,1,2,0:T(8,128)(2,1)} %get-tuple-element.306, ...), kind=kOutput, calls=%fused_computation.9.clone.1 | convolution fusion | flops 544210944 | bytes 12746756 | tf_op jit(solution)/shard_map/while/body/eval_jaxpr/kgps,skd->kgpd/dot_general | solution.py:53
  184.6 2.6 bitcast_reduce_fusion.2
  187.2 1.4 fusion.263
  188.6 3.3 %bitcast_add_fusion.6 = f32[1,8,512,128]{3,2,1,0:T(8,128)S(1)} fusion(f32[1,8,512,128]{3,2,1,0:T(8,128)S(1)} %get-tuple-element.295, f32[512,512,8]{1,0,2:T(8,128)S(1)} %get-tuple-element.282, f32[8,512]{1,0:T(8,128)S(1)} %bitcast.657, f32[8,512]{1,0:T(8,128)S(1)} %get-tuple-element.283, bf16[8,512,1,128]{3,1,2,0:T(8,128)(2,1)} %get-tuple-element.306, ...), kind=kOutput, calls=%fused_computation.9.clone.1 | convolution fusion | flops 544210944 | bytes 12746756 | tf_op jit(solution)/shard_map/while/body/eval_jaxpr/kgps,skd->kgpd/dot_general | solution.py:53
  191.9 2.6 bitcast_reduce_fusion.2
  194.5 1.4 fusion.263
  196.0 3.3 %bitcast_add_fusion.6 = f32[1,8,512,128]{3,2,1,0:T(8,128)S(1)} fusion(f32[1,8,512,128]{3,2,1,0:T(8,128)S(1)} %get-tuple-element.295, f32[512,512,8]{1,0,2:T(8,128)S(1)} %get-tuple-element.282, f32[8,512]{1,0:T(8,128)S(1)} %bitcast.657, f32[8,512]{1,0:T(8,128)S(1)} %get-tuple-element.283, bf16[8,512,1,128]{3,1,2,0:T(8,128)(2,1)} %get-tuple-element.306, ...), kind=kOutput, calls=%fused_computation.9.clone.1 | convolution fusion | flops 544210944 | bytes 12746756 | tf_op jit(solution)/shard_map/while/body/eval_jaxpr/kgps,skd->kgpd/dot_general | solution.py:53
  199.3 2.6 bitcast_reduce_fusion.2
  201.9 1.4 fusion.263
  203.3 3.3 %bitcast_add_fusion.6 = f32[1,8,512,128]{3,2,1,0:T(8,128)S(1)} fusion(f32[1,8,512,128]{3,2,1,0:T(8,128)S(1)} %get-tuple-element.295, f32[512,512,8]{1,0,2:T(8,128)S(1)} %get-tuple-element.282, f32[8,512]{1,0:T(8,128)S(1)} %bitcast.657, f32[8,512]{1,0:T(8,128)S(1)} %get-tuple-element.283, bf16[8,512,1,128]{3,1,2,0:T(8,128)(2,1)} %get-tuple-element.306, ...), kind=kOutput, calls=%fused_computation.9.clone.1 | convolution fusion | flops 544210944 | bytes 12746756 | tf_op jit(solution)/shard_map/while/body/eval_jaxpr/kgps,skd->kgpd/dot_general | solution.py:53
  208.6 1.2 select_convert_fusion
  209.8 4.7 %collective-permute-start.1 = (bf16[2,512,128]{2,1,0:T(8,128)(2,1)}, bf16[2,512,128]{2,1,0:T(8,128)(2,1)S(1)}, u32[]{:S(2)}, u32[]{:S(2)}) collective-permute-start(bf16[2,512,128]{2,1,0:T(8,128)(2,1)} %collective-permute-done), channel_id=1, source_target_pairs={{0,16},{16,32},{32,48},{48,64},{64,80},{80,96},{96,112},{1,17},{17... | collective-permute-start | bytes 786440 | tf_op jit(solution)/shard_map/ppermute | solution.py:15
  214.5 1.7 fusion.44
  216.2 6.6 %collective-permute-done.1 = bf16[2,512,128]{2,1,0:T(8,128)(2,1)S(1)} collective-permute-done((bf16[2,512,128]{2,1,0:T(8,128)(2,1)}, bf16[2,512,128]{2,1,0:T(8,128)(2,1)S(1)}, u32[]{:S(2)}, u32[]{:S(2)}) %collective-permute-start.1) | collective-permute-done | bytes 262176 | tf_op jit(solution)/shard_map/ppermute | solution.py:15
  222.8 3.8 %collective-permute-start.2 = (bf16[2,512,128]{2,1,0:T(8,128)(2,1)S(1)}, bf16[2,512,128]{2,1,0:T(8,128)(2,1)S(1)}, u32[]{:S(2)}, u32[]{:S(2)}) collective-permute-start(bf16[2,512,128]{2,1,0:T(8,128)(2,1)S(1)} %collective-permute-done.1), channel_id=1, source_target_pairs={{0,16},{16,32},{32,48},{48,64},{64,80},{80,96},{96,112},{1,17},{17... | collective-permute-start | bytes 786440 | tf_op jit(solution)/shard_map/ppermute | solution.py:15
  227.3 7.3 %collective-permute-done.2 = bf16[2,512,128]{2,1,0:T(8,128)(2,1)S(1)} collective-permute-done((bf16[2,512,128]{2,1,0:T(8,128)(2,1)S(1)}, bf16[2,512,128]{2,1,0:T(8,128)(2,1)S(1)}, u32[]{:S(2)}, u32[]{:S(2)}) %collective-permute-start.2) | collective-permute-done | bytes 262176 | tf_op jit(solution)/shard_map/ppermute | solution.py:15
  234.7 2.9 collective-permute-start.3
  238.4 7.3 %collective-permute-done.3 = bf16[2,512,128]{2,1,0:T(8,128)(2,1)S(1)} collective-permute-done((bf16[2,512,128]{2,1,0:T(8,128)(2,1)S(1)}, bf16[2,512,128]{2,1,0:T(8,128)(2,1)S(1)}, u32[]{:S(2)}, u32[]{:S(2)}) %collective-permute-start.3) | collective-permute-done | bytes 262176 | tf_op jit(solution)/shard_map/ppermute | solution.py:15
  245.7 2.0 collective-permute-start.4
  248.5 7.9 %collective-permute-done.4 = bf16[2,512,128]{2,1,0:T(8,128)(2,1)S(1)} collective-permute-done((bf16[2,512,128]{2,1,0:T(8,128)(2,1)S(1)}, bf16[2,512,128]{2,1,0:T(8,128)(2,1)S(1)}, u32[]{:S(2)}, u32[]{:S(2)}) %collective-permute-start.4) | collective-permute-done | bytes 262176 | tf_op jit(solution)/shard_map/ppermute | solution.py:15
  256.3 1.9 collective-permute-start.5
  259.0 8.0 %collective-permute-done.5 = bf16[2,512,128]{2,1,0:T(8,128)(2,1)S(1)} collective-permute-done((bf16[2,512,128]{2,1,0:T(8,128)(2,1)S(1)}, bf16[2,512,128]{2,1,0:T(8,128)(2,1)S(1)}, u32[]{:S(2)}, u32[]{:S(2)}) %collective-permute-start.5) | collective-permute-done | bytes 262176 | tf_op jit(solution)/shard_map/ppermute | solution.py:15
  267.0 2.1 collective-permute-start.6
  269.9 7.8 %collective-permute-done.6 = bf16[2,512,128]{2,1,0:T(8,128)(2,1)S(1)} collective-permute-done((bf16[2,512,128]{2,1,0:T(8,128)(2,1)S(1)}, bf16[2,512,128]{2,1,0:T(8,128)(2,1)S(1)}, u32[]{:S(2)}, u32[]{:S(2)}) %collective-permute-start.6) | collective-permute-done | bytes 262176 | tf_op jit(solution)/shard_map/ppermute | solution.py:15
  278.4 1.7 fusion.65
  280.1 1.7 fusion.61
  281.8 1.7 fusion.57
  284.0 1.7 fusion.53
  285.8 2.0 fusion.145
  287.8 1.9 fusion.124
  291.5 1.2 fusion.133
  293.7 1.2 copy-done.3
  295.0 1.0 fusion.139
  296.9 1.0 copy.144
  (95 shorter events, 18.7 us)
Async XLA Ops:
  7.2 77.6 %copy-start = (bf16[512,512]{1,0:T(8,128)(2,1)S(1)}, bf16[512,512]{1,0:T(8,128)(2,1)}, u32[]{:S(2)}) copy-start(bf16[512,512]{1,0:T(8,128)(2,1)} %param.26) | copy-start | bytes 1572868
  7.2 46.0 %all-gather.7.cloned.1.call-start = ((), (), s32[]{:S(2)}) async-start(), calls=%async_computation.3 | async-start | bytes 1114112 | tf_op jit(solution)/shard_map/all_gather | solution.py:94
  7.9 71.0 %all-gather.5.cloned.1.call-start = ((), (), s32[]{:S(2)}) async-start(), calls=%async_computation.2 | async-start | bytes 1114112 | tf_op jit(solution)/shard_map/all_gather | solution.py:93
  10.1 14.5 %all-to-all-start = ((bf16[32,8,128]{2,0,1:T(8,128)(2,1)}), bf16[32,8,128]{2,0,1:T(8,128)(2,1)S(1)}, u32[]{:S(2)}, u32[]{:S(2)}) async-start(bf16[32,8,128]{2,0,1:T(8,128)(2,1)} %copy_bitcast_fusion.1), calls=%async_computation | async-start | bytes 131072 | tf_op jit(solution)/shard_map/all_to_all | solution.py:142
  24.7 4.7 %copy-start.5 = (bf16[32,8,128]{2,0,1:T(8,128)(2,1)}, bf16[32,8,128]{2,0,1:T(8,128)(2,1)S(1)}, u32[]{:S(2)}) copy-start(bf16[32,8,128]{2,0,1:T(8,128)(2,1)S(1)} %all-to-all-done) | copy-start | bytes 196612
  24.7 15.8 %all-to-all-start.1 = ((bf16[32,8,128]{2,0,1:T(8,128)(2,1)}), bf16[32,8,128]{2,0,1:T(8,128)(2,1)S(1)}, u32[]{:S(2)}, u32[]{:S(2)}) async-start(bf16[32,8,128]{2,0,1:T(8,128)(2,1)} %copy_bitcast_fusion), calls=%async_computation.1 | async-start | bytes 131072 | tf_op jit(solution)/shard_map/all_to_all | solution.py:143
  29.4 84.3 %all-gather.9.cloned.1.call-start = ((), (), s32[]{:S(2)}) async-start(), calls=%async_computation.4 | async-start | bytes 1114112 | tf_op jit(solution)/shard_map/all_gather | solution.py:148
  30.1 117.6 %all-gather.11.cloned.1.call-start = ((), (), s32[]{:S(2)}) async-start(), calls=%async_computation.5 | async-start | bytes 1114112 | tf_op jit(solution)/shard_map/all_gather | solution.py:149
  40.5 0.6 copy-start.6
  41.2 5.3 %copy-start.4 = (bf16[1,512,1024]{2,1,0:T(8,128)(2,1)S(1)}, bf16[1,512,1024]{2,1,0:T(8,128)(2,1)}, u32[]{:S(2)}) copy-start(bf16[1,512,1024]{2,1,0:T(8,128)(2,1)} %param.29) | copy-start | bytes 3145732
  46.4 2.0 copy-start.7
  79.8 130.0 %collective-permute-start = (bf16[2,512,128]{2,1,0:T(8,128)(2,1)S(1)}, bf16[2,512,128]{2,1,0:T(8,128)(2,1)}, u32[]{:S(2)}, u32[]{:S(2)}) collective-permute-start(bf16[2,512,128]{2,1,0:T(8,128)(2,1)S(1)} %pad_maximum_fusion), channel_id=1, source_target_pairs={{0,16},{16,32},{32,48},{48,64},{64,80},{80,96},{96,112},{1,17},{17... | collective-permute-start | bytes 786440 | tf_op jit(solution)/shard_map/ppermute | solution.py:15
  209.8 12.9 %collective-permute-start.1 = (bf16[2,512,128]{2,1,0:T(8,128)(2,1)}, bf16[2,512,128]{2,1,0:T(8,128)(2,1)S(1)}, u32[]{:S(2)}, u32[]{:S(2)}) collective-permute-start(bf16[2,512,128]{2,1,0:T(8,128)(2,1)} %collective-permute-done), channel_id=1, source_target_pairs={{0,16},{16,32},{32,48},{48,64},{64,80},{80,96},{96,112},{1,17},{17... | collective-permute-start | bytes 786440 | tf_op jit(solution)/shard_map/ppermute | solution.py:15
  222.8 11.9 %collective-permute-start.2 = (bf16[2,512,128]{2,1,0:T(8,128)(2,1)S(1)}, bf16[2,512,128]{2,1,0:T(8,128)(2,1)S(1)}, u32[]{:S(2)}, u32[]{:S(2)}) collective-permute-start(bf16[2,512,128]{2,1,0:T(8,128)(2,1)S(1)} %collective-permute-done.1), channel_id=1, source_target_pairs={{0,16},{16,32},{32,48},{48,64},{64,80},{80,96},{96,112},{1,17},{17... | collective-permute-start | bytes 786440 | tf_op jit(solution)/shard_map/ppermute | solution.py:15
  234.7 11.0 %collective-permute-start.3 = (bf16[2,512,128]{2,1,0:T(8,128)(2,1)S(1)}, bf16[2,512,128]{2,1,0:T(8,128)(2,1)S(1)}, u32[]{:S(2)}, u32[]{:S(2)}) collective-permute-start(bf16[2,512,128]{2,1,0:T(8,128)(2,1)S(1)} %collective-permute-done.2), channel_id=1, source_target_pairs={{0,16},{16,32},{32,48},{48,64},{64,80},{80,96},{96,112},{1,17},{17... | collective-permute-start | bytes 786440 | tf_op jit(solution)/shard_map/ppermute | solution.py:15
  245.7 10.7 %collective-permute-start.4 = (bf16[2,512,128]{2,1,0:T(8,128)(2,1)S(1)}, bf16[2,512,128]{2,1,0:T(8,128)(2,1)S(1)}, u32[]{:S(2)}, u32[]{:S(2)}) collective-permute-start(bf16[2,512,128]{2,1,0:T(8,128)(2,1)S(1)} %collective-permute-done.3), channel_id=1, source_target_pairs={{0,16},{16,32},{32,48},{48,64},{64,80},{80,96},{96,112},{1,17},{17... | collective-permute-start | bytes 786440 | tf_op jit(solution)/shard_map/ppermute | solution.py:15
  256.3 10.7 %collective-permute-start.5 = (bf16[2,512,128]{2,1,0:T(8,128)(2,1)S(1)}, bf16[2,512,128]{2,1,0:T(8,128)(2,1)S(1)}, u32[]{:S(2)}, u32[]{:S(2)}) collective-permute-start(bf16[2,512,128]{2,1,0:T(8,128)(2,1)S(1)} %collective-permute-done.4), channel_id=1, source_target_pairs={{0,16},{16,32},{32,48},{48,64},{64,80},{80,96},{96,112},{1,17},{17... | collective-permute-start | bytes 786440 | tf_op jit(solution)/shard_map/ppermute | solution.py:15
  267.0 10.7 %collective-permute-start.6 = (bf16[2,512,128]{2,1,0:T(8,128)(2,1)S(1)}, bf16[2,512,128]{2,1,0:T(8,128)(2,1)S(1)}, u32[]{:S(2)}, u32[]{:S(2)}) collective-permute-start(bf16[2,512,128]{2,1,0:T(8,128)(2,1)S(1)} %collective-permute-done.5), channel_id=1, source_target_pairs={{0,16},{16,32},{32,48},{48,64},{64,80},{80,96},{96,112},{1,17},{17... | collective-permute-start | bytes 786440 | tf_op jit(solution)/shard_map/ppermute | solution.py:15
  269.9 10.2 %copy-start.2 = (f32[512,512,4]{1,0,2:T(8,128)}, f32[512,512,4]{1,0,2:T(8,128)S(1)}, u32[]{:S(2)}) copy-start(f32[512,512,4]{1,0,2:T(8,128)S(1)} %get-tuple-element.208) | copy-start | bytes 12582916
  281.8 2.2 copy-start.1
  292.8 2.2 copy-start.3
Sparse Core Ops, SparseCore 0:
  9.7 34.8 all-gather.6
  46.3 32.4 all-gather.4
  81.2 32.4 all-gather.8
  115.2 32.5 all-gather.10
where the time goes:
time: 306 us; the launch traced here: 304 us
  waiting for transfers between devices  136 us (44%)
  matrix products  78.2 us (26%)
  starting transfers between devices  35.5 us (12%)
  other arithmetic  26.3 us (9%)
  between operations  14.9 us (5%)
  local copies, waits for them, and re-layouts  13.2 us (4%)
    ppermute x7, waiting for transfers between devices, from_behind(): return lax.ppermute(block, axis, route)  44.9 us
    dot_general x17, matrix products, attend_block(): jnp.einsum('kgps,skd->kgpd', weights.astype(jnp.bfloat16), value_rows, pr...  41.2 us
    dot_general x17, matrix products, attend_block(): jnp.einsum('pkgd,skd->kgps', queries, key_rows, preferred_element_type=jn...  36 us
    all_gather x1, waiting for transfers between devices, on_device(): lax.all_gather(sent_v, 'resp', axis=0, tiled=True)  34.1 us
    all_gather x1, waiting for transfers between devices, on_device(): lax.all_gather(sent_k, 'resp', axis=0, tiled=True)  25.2 us
    all_gather x1, waiting for transfers between devices, on_device(): lax.all_gather(k_prompt, 'resp', axis=0, tiled=True)  24.7 us
    reduce_sum x13, other arithmetic, attend_block(): run_sum = run_sum * rescale + jnp.sum(weights, axis=-1)  23 us
    ppermute x7, starting transfers between devices, from_behind(): return lax.ppermute(block, axis, route)  22.5 us
  transfers between devices with their start and end apart: 13, of which 10 were waited for; matrix products, arithmetic and copies ran while one was open for 32% of the time, Pallas kernels for 0%

commit v1 on v0

v1 whole, which is shorter than its diff:
```python
import functools

import jax
import jax.numpy as jnp
from jax import lax
from jax.experimental import pallas as pl
from jax.experimental.pallas import tpu as pltpu
from jax.sharding import PartitionSpec as P

QH = 64
KVH = 8
HD = 128
RBLK = 8
ROWS = 512
SUB = 32
GROUP = QH // KVH
SCALE = HD**-0.5 * 1.4426950408889634
LOW, HIGH = 1e-18, 1e30
AXES = ("chain", "resp")
STEPS = (0, 1, 3, 2)
MIB = 2**20
PLACES = [(y, z, x, k) for y in range(4) for z in range(4) for x in range(4) for k in range(2)]


def device_at(y, z, x, core):
    return (y * 2 + z // 2) * 16 + (x * 2 + z % 2) * 2 + core


def move(block, target):
    route = [(device_at(*p), device_at(*target(*p))) for p in PLACES]
    return lax.ppermute(block, AXES, route)


def move_back(block, target):
    route = [(device_at(*target(*p)), device_at(*p)) for p in PLACES]
    return lax.ppermute(block, AXES, route)


def along_y(d):
    return lambda y, z, x, core: ((y + d) % 4, z, x, core)


def along_z(d):
    return lambda y, z, x, core: (y, (z + d) % 4, x, core)


def along_x(d):
    return lambda y, z, x, core: (y, z, (x + d) % 4, core)


def other_core(y, z, x, core):
    return (y, z, x, 1 - core)


def query_home(half):
    def target(y, z, x, core):
        hi, lo = z // 2, z % 2
        if half:
            y, hi = 3 - y, 1 - hi
        return (x, lo * 2 + hi, (y + x) % 4, core)

    return target


def dot_t(a, b):
    return lax.dot_general(a, b, (((1,), (1,)), ((), ())), preferred_element_type=jnp.float32)


def fold_rows(p):
    return jnp.sum(p.reshape(p.shape[0] // 8, 8, p.shape[1]), axis=0)


def token_rows(block):
    return block.reshape(-1, HD)


def online(carried, keys, values_t, queries, visible):
    run_max, run_sum, run_acc = carried
    scores = dot_t(keys, queries) * SCALE
    if visible is not None:
        scores = jnp.where(visible, scores, -1e30)
    new_max = jnp.maximum(run_max, jnp.max(scores, axis=0, keepdims=True))
    weights = jnp.exp2(scores - new_max)
    if visible is not None:
        weights = jnp.where(visible, weights, 0.0)
    rescale = jnp.exp2(run_max - new_max)
    run_sum = run_sum * rescale + jnp.sum(weights, axis=0, keepdims=True)
    added = jnp.dot(values_t, weights.astype(jnp.bfloat16), preferred_element_type=jnp.float32)
    return (new_max, run_sum, run_acc * rescale + added)


def fresh(cols):
    return (
        jnp.full((1, cols), -1e30, jnp.float32),
        jnp.zeros((1, cols), jnp.float32),
        jnp.zeros((HD, cols), jnp.float32),
    )


def tree_seen(tree_ref, len_ref):
    lines = []
    for j in range(RBLK):
        parent = tree_ref[0, j]
        line = jnp.int32(1 << j)
        for i in range(j):
            line = line | jnp.where(parent == i, lines[i], 0)
        lines.append(line)
    key_at = lax.broadcasted_iota(jnp.int32, (ROWS, ROWS), 0)
    row_at = lax.broadcasted_iota(jnp.int32, (ROWS, ROWS), 1)
    span = ROWS // RBLK
    line_of_row = jnp.zeros((ROWS, ROWS), jnp.int32)
    for j in range(RBLK):
        line_of_row = jnp.where(row_at // span == j, lines[j], line_of_row)
    related = (lax.shift_right_logical(line_of_row, key_at // span) & 1) == 1
    return related & (key_at <= row_at) & (key_at < len_ref[0])


def own_kernel(tree_ref, len_ref, q_ref, k_ref, v_ref, acc_ref, sum_ref, seen, vt):
    @pl.when(pl.program_id(0) == 0)
    def _():
        seen[...] = jnp.where(tree_seen(tree_ref, len_ref), 0.0, -jnp.inf)
        vt[...] = v_ref[...].T

    weights = jnp.exp2(dot_t(k_ref[...], q_ref[...]) * SCALE + seen[...])
    sum_ref[0] = fold_rows(weights)
    acc_ref[0] = jnp.dot(vt[...], weights.astype(jnp.bfloat16), preferred_element_type=jnp.float32)


def load_chunks(parts, kb, vt):
    at = 0
    for part in parts:
        keys, values = token_rows(part[:, 0]), token_rows(part[:, 1])
        count = keys.shape[0]
        kb[at : at + count, :] = keys
        vt[:, at : at + count] = values.T
        at += count


def chunk_kernel(part_count, *refs):
    q_ref, acc_in, sum_in = refs[:3]
    parts = refs[3 : 3 + part_count]
    acc_ref, sum_ref, kb, vt = refs[3 + part_count :]

    @pl.when(pl.program_id(0) == 0)
    def _():
        load_chunks(parts, kb, vt)

    weights = jnp.exp2(dot_t(kb[...], q_ref[...]) * SCALE)
    sum_ref[0] = sum_in[0] + fold_rows(weights)
    acc_ref[0] = acc_in[0] + jnp.dot(
        vt[...], weights.astype(jnp.bfloat16), preferred_element_type=jnp.float32
    )


def last_kernel(part_count, slabs, *refs):
    tree_ref, len_ref, q_ref, acc_in, sum_in = refs[:5]
    parts = refs[5 : 5 + part_count]
    refs = refs[5 + part_count :]
    q_all, k_own, v_own = refs[:3]
    held = refs[3 : 3 + len(slabs)]
    out_ref, kb, vt, low, high, slab, q_buf, own_buf = refs[3 + len(slabs) :]
    head = pl.program_id(0)

    @pl.when(head == 0)
    def _():
        load_chunks(parts, kb, vt)
        low[...] = jnp.full_like(low, 1.0)
        high[...] = jnp.full_like(high, 1.0)

    live = lax.broadcasted_iota(jnp.int32, (ROWS, HD), 0) < len_ref[0]
    weights = jnp.exp2(dot_t(kb[...], q_ref[...]) * SCALE)
    total = jnp.sum(sum_in[0] + fold_rows(weights), axis=0, keepdims=True)
    acc = acc_in[0] + jnp.dot(
        vt[...], weights.astype(jnp.bfloat16), preferred_element_type=jnp.float32
    )
    low[...] = jnp.minimum(low[...], total)
    high[...] = jnp.maximum(high[...], total)
    cols = pl.ds(pl.multiple_of(head * HD, HD), HD)
    out_ref[:, cols] = jnp.where(live, (acc / total).T, 0.0).astype(jnp.bfloat16)

    @pl.when(head == pl.num_programs(0) - 1)
    def _():
        good = (jnp.min(low[...]) > LOW) & (jnp.max(high[...]) < HIGH)

        @pl.when(jnp.logical_not(good))
        def _():
            pltpu.sync_copy(k_own, own_buf.at[0])
            pltpu.sync_copy(v_own, own_buf.at[1])

            def one_head(h, unused):
                at = pl.multiple_of(h * HD, HD)
                pltpu.sync_copy(q_all.at[:, pl.ds(at, HD)], q_buf)
                queries = q_buf[...]
                carried = fresh(ROWS)
                for ref, spots in zip(held, slabs):
                    for spot in range(spots):
                        pltpu.sync_copy(ref.at[pl.ds(spot * 16, 16)], slab)
                        carried = online(
                            carried, token_rows(slab[:, 0]), token_rows(slab[:, 1]).T, queries, None
                        )
                seen = tree_seen(tree_ref, len_ref)
                run_max, run_sum, run_acc = online(
                    carried, own_buf[0], own_buf[1].T, queries, seen
                )
                shown = jnp.where(live, (run_acc / run_sum).T, 0.0)
                out_ref[:, pl.ds(at, HD)] = shown.astype(jnp.bfloat16)
                return unused

            lax.fori_loop(0, GROUP, one_head, 0)


def prompt_kernel(place_ref, qa_ref, qb_ref, *refs):
    here, here_s, wide, wide_s, far, far_s = refs[:6]
    outs = refs[6:8]
    kb, vb, vt, qs, acc, total = refs[8:]
    y, z, x, core = (place_ref[i] for i in range(4))
    half = ROWS // 2
    heads = GROUP // 2
    wide_cols = heads * half

    def place(ref, at, z_step, y_step, x_from, core_from):
        y0 = (y - y_step) % 4
        z0 = (z - z_step) % 4
        block = (y0 * 2 + z0 // 2) * 16 + (x_from * 2 + z0 % 2) * 2 + core_from
        spot = pl.ds(pl.multiple_of(block * SUB, SUB), SUB)
        kb[spot, :] = ref[at, 0]
        vb[spot, :] = ref[at, 1]

    for ref, wide_ref, far_ref, core_from in (
        (here, wide, far, core),
        (here_s, wide_s, far_s, 1 - core),
    ):
        for i, z_step in enumerate(STEPS):
            for j, y_step in enumerate(STEPS):
                at = i * 4 + j
                place(ref, at, z_step, y_step, x, core_from)
                place(wide_ref, at, z_step, y_step, (x + 3) % 4, core_from)
                place(wide_ref, 16 + at, z_step, y_step, (x + 1) % 4, core_from)
                place(far_ref, at, z_step, y_step, (x + 2) % 4, core_from)
    for b in range(8):
        vt[b] = vb[b * ROWS : (b + 1) * ROWS, :].T
    for side, q_ref in enumerate((qa_ref, qb_ref)):
        for h in range(heads):
            qs[side, h * half : (h + 1) * half, :] = q_ref[:, h * HD : (h + 1) * HD]

    block_a = ((x - y) % 4) * 2 + z % 2
    blocks = (block_a, 7 - block_a)

    def key_rows(block, count):
        return kb[pl.ds(pl.multiple_of(block * ROWS, ROWS), count), :]

    for side, count in ((0, half), (1, ROWS)):
        scores = dot_t(key_rows(blocks[side], count), qs[side]) * SCALE
        key_at = lax.broadcasted_iota(jnp.int32, scores.shape, 0)
        row_at = lax.broadcasted_iota(jnp.int32, scores.shape, 1) % half + side * half
        weights = jnp.where(key_at <= row_at, jnp.exp2(scores), 0.0)
        total[side] = fold_rows(weights)
        acc[side] = jnp.dot(
            vt[blocks[side]][:, :count],
            weights.astype(jnp.bfloat16),
            preferred_element_type=jnp.float32,
        )
    for n in range(7):
        first = n < block_a
        side = jnp.where(first, 0, 1)
        block = jnp.where(first, n, n - block_a)
        weights = jnp.exp2(dot_t(key_rows(block, ROWS), qs[side]) * SCALE)
        total[side] += fold_rows(weights)
        acc[side] += jnp.dot(
            vt[block], weights.astype(jnp.bfloat16), preferred_element_type=jnp.float32
        )

    def store(side, sums, accs):
        shown = accs / sums
        for h in range(heads):
            outs[side][:, h * HD : (h + 1) * HD] = shown[:, h * half : (h + 1) * half].T.astype(
                jnp.bfloat16
            )

    sums = [jnp.sum(total[side], axis=0, keepdims=True) for side in range(2)]
    for side in range(2):
        store(side, sums[side], acc[side])
    least = jnp.min(jnp.minimum(sums[0], sums[1]))
    most = jnp.max(jnp.maximum(sums[0], sums[1]))
    good = (least > LOW) & (most < HIGH)

    @pl.when(jnp.logical_not(good))
    def _():
        for side in range(2):

            def one_block(b, carried, side=side):
                key_at = lax.broadcasted_iota(jnp.int32, (ROWS, wide_cols), 0) + b * ROWS
                row_at = lax.broadcasted_iota(jnp.int32, (ROWS, wide_cols), 1) % half
                row_at = row_at + side * half + blocks[side] * ROWS
                return online(carried, key_rows(b, ROWS), vt[b], qs[side], key_at <= row_at)

            run_max, run_sum, run_acc = lax.fori_loop(
                0, blocks[side] + 1, one_block, fresh(wide_cols)
            )
            store(side, run_sum, run_acc)


def whole(shape):
    return pl.BlockSpec(shape, lambda h: (0,) * len(shape))


STATE = (
    jax.ShapeDtypeStruct((GROUP, HD, ROWS), jnp.float32),
    jax.ShapeDtypeStruct((GROUP, 8, ROWS), jnp.float32),
)
STATE_SPECS = (
    pl.BlockSpec((1, HD, ROWS), lambda h: (h, 0, 0)),
    pl.BlockSpec((1, 8, ROWS), lambda h: (h, 0, 0)),
)
HEAD_SPEC = pl.BlockSpec((ROWS, HD), lambda h: (0, h))
SCALAR = pl.BlockSpec(memory_space=pltpu.SMEM)
PARAMS = dict(compiler_params=pltpu.CompilerParams(vmem_limit_bytes=48 * MIB))


def cost(rows, keys):
    return pl.CostEstimate(
        flops=8 * rows * keys * HD, bytes_accessed=6 * MIB, transcendentals=rows * keys
    )


def attend_own(tree, length, q, k, v):
    return pl.pallas_call(
        own_kernel,
        grid=(GROUP,),
        in_specs=[SCALAR, SCALAR, HEAD_SPEC, whole((ROWS, HD)), whole((ROWS, HD))],
        out_specs=STATE_SPECS,
        out_shape=STATE,
        scratch_shapes=[
            pltpu.VMEM((ROWS, ROWS), jnp.float32),
            pltpu.VMEM((HD, ROWS), jnp.bfloat16),
        ],
        cost_estimate=cost(GROUP * ROWS, ROWS),
        name="own_keys",
        **PARAMS,
    )(tree, length, q, k, v)


def attend_chunk(q, state, parts, name):
    tokens = sum(part.shape[0] for part in parts) * SUB
    return pl.pallas_call(
        functools.partial(chunk_kernel, len(parts)),
        grid=(GROUP,),
        in_specs=[HEAD_SPEC, *STATE_SPECS] + [whole(part.shape) for part in parts],
        out_specs=STATE_SPECS,
        out_shape=STATE,
        scratch_shapes=[
            pltpu.VMEM((tokens, HD), jnp.bfloat16),
            pltpu.VMEM((HD, tokens), jnp.bfloat16),
        ],
        cost_estimate=cost(GROUP * ROWS, tokens),
        name=name,
        **PARAMS,
    )(q, *state, *parts)


def attend_last(tree, length, q, state, parts, k_own, v_own, held):
    tokens = sum(part.shape[0] for part in parts) * SUB
    slabs = tuple(part.shape[0] // 16 for part in held)
    anywhere = pl.BlockSpec(memory_space=pl.ANY)
    return pl.pallas_call(
        functools.partial(last_kernel, len(parts), slabs),
        grid=(GROUP,),
        in_specs=[SCALAR, SCALAR, HEAD_SPEC, *STATE_SPECS]
        + [whole(part.shape) for part in parts]
        + [anywhere] * (3 + len(held)),
        out_specs=whole((ROWS, GROUP * HD)),
        out_shape=jax.ShapeDtypeStruct((ROWS, GROUP * HD), jnp.bfloat16),
        scratch_shapes=[
            pltpu.VMEM((tokens, HD), jnp.bfloat16),
            pltpu.VMEM((HD, tokens), jnp.bfloat16),
            pltpu.VMEM((1, ROWS), jnp.float32),
            pltpu.VMEM((1, ROWS), jnp.float32),
            pltpu.VMEM((16, 2, SUB, HD), jnp.bfloat16),
            pltpu.VMEM((ROWS, HD), jnp.bfloat16),
            pltpu.VMEM((2, ROWS, HD), jnp.bfloat16),
        ],
        cost_estimate=cost(GROUP * ROWS, tokens),
        name="last_keys",
        **PARAMS,
    )(tree, length, q, *state, *parts, q, k_own, v_own, *held)


def attend_prompt(place, qa, qb, held):
    half = ROWS // 2
    vmem = pl.BlockSpec(memory_space=pltpu.VMEM)
    cols = GROUP // 2 * half
    return pl.pallas_call(
        prompt_kernel,
        in_specs=[SCALAR] + [vmem] * (2 + len(held)),
        out_specs=[vmem, vmem],
        out_shape=[jax.ShapeDtypeStruct(qa.shape, jnp.bfloat16)] * 2,
        scratch_shapes=[
            pltpu.VMEM((8 * ROWS, HD), jnp.bfloat16),
            pltpu.VMEM((8 * ROWS, HD), jnp.bfloat16),
            pltpu.VMEM((8, HD, ROWS), jnp.bfloat16),
            pltpu.VMEM((2, cols, HD), jnp.bfloat16),
            pltpu.VMEM((2, HD, cols), jnp.float32),
            pltpu.VMEM((2, 8, cols), jnp.float32),
        ],
        cost_estimate=cost(cols, 9 * ROWS),
        name="prompt_rows",
        **PARAMS,
    )(place, qa, qb, *held)


def pick(block, index, axis=0):
    return lax.dynamic_index_in_dim(block, index, axis, False)


def on_device(q_prompt, k_prompt, v_prompt, q_resp, k_resp, v_resp, tree_table, lengths):
    chain, resp = lax.axis_index("chain"), lax.axis_index("resp")
    y, z, x, core = chain // 2, chain % 2 * 2 + resp // 2 % 2, resp // 4, resp % 2
    place = jnp.stack([y, z, x, core]).astype(jnp.int32)
    half = ROWS // 2
    q = q_resp[0]

    pieces = jnp.stack([k_prompt.reshape(SUB, KVH, HD), v_prompt.reshape(SUB, KVH, HD)])
    pieces = pieces.transpose(2, 0, 1, 3).reshape(4, 2, 2, SUB, HD)
    over_y = [pick(pieces, y)]
    over_y += [move(pick(pieces, (y + d) % 4), along_y(d)) for d in STEPS[1:]]
    over_y = jnp.stack(over_y)
    over_z = [pick(over_y, z // 2, 1)]
    over_z += [move(pick(over_y, (z + d) % 4 // 2, 1), along_z(d)) for d in STEPS[1:]]
    here = jnp.concatenate(over_z)
    here_s = move(here, other_core)
    from_left, from_right = move(here, along_x(1)), move(here, along_x(3))
    wide = jnp.concatenate([from_left, from_right])
    wide_s = move(wide, other_core)
    far = jnp.concatenate([move(from_left[:8], along_x(1)), move(from_right[8:], along_x(3))])
    far_s = move(far, other_core)

    qa = move(q_prompt[:half], query_home(0))
    qb = move(q_prompt[half:], query_home(1))

    state = attend_own(tree_table, lengths, q, k_resp[0], v_resp[0])
    state = attend_chunk(q, state, (here, here_s), "here_keys")
    held = (here, here_s, wide, wide_s, far, far_s)
    out_a, out_b = attend_prompt(place, qa, qb, held)
    out_a = move_back(out_a, query_home(0))
    out_b = move_back(out_b, query_home(1))
    prompt_out = jnp.concatenate([out_a, out_b])
    state = attend_chunk(q, state, (wide, wide_s), "wide_keys")
    resp_out = attend_last(
        tree_table, lengths, q, state, (far, far_s), k_resp[0], v_resp[0], held
    )
    return (prompt_out, resp_out[None])


def solution(mesh):
    placed = (
        P("chain", "resp"),
        P(("chain", "resp"), None),
        P(("chain", "resp"), None),
        P("resp", None, "chain"),
        P("resp", None, "chain"),
        P("resp", None, "chain"),
        P("resp", None),
        P("resp"),
    )
    return jax.shard_map(
        on_device,
        mesh=mesh,
        in_specs=placed,
        out_specs=(P("chain", "resp"), P("resp", None, "chain")),
        check_vma=False,
    )
```

time: 306 us -> 149 us (0.49)
  the two profiles are of different devices: /device:TPU:8 before, /device:TPU:1 now
where the time goes in v1:
time: 149 us
  Pallas kernels  94.4 us (63%)
  starting transfers between devices  43.8 us (29%)
  waiting for transfers between devices  4.82 us (3%)
  local copies, waits for them, and re-layouts  3.37 us (2%)
  between operations  1.68 us (1%)
    pallas_call x1, Pallas kernels, attend_last(): pl.pallas_call(functools.partial(last_kernel, len(parts), slabs), grid=(G...  57 us
    ppermute x15, starting transfers between devices, move(): return lax.ppermute(block, AXES, route)  30.2 us
    pallas_call x1, Pallas kernels, attend_prompt(): pl.pallas_call(prompt_kernel, in_specs=[SCALAR] + [vmem] * (2 + len(held)...  17.4 us
    pallas_call x2, Pallas kernels, attend_chunk(): pl.pallas_call(functools.partial(chunk_kernel, len(parts)), grid=(GROUP,)...  14.8 us
    ppermute x2, starting transfers between devices, move_back(): return lax.ppermute(block, AXES, route)  13.6 us
    pallas_call x1, Pallas kernels, attend_own(): pl.pallas_call(own_kernel, grid=(GROUP,), in_specs=[SCALAR, SCALAR, HEAD_...  5.15 us
    ppermute x15, waiting for transfers between devices, move(): return lax.ppermute(block, AXES, route)  4.82 us
    unnamed x16, local copies, waits for them, and re-layouts  3.19 us
  transfers between devices with their start and end apart: 17, of which 2 were waited for; matrix products, arithmetic and copies ran while one was open for 0% of the time, Pallas kernels for 52%

profile of v1, /device:TPU:1, one launch (start us, length us, event | category | flops | bytes accessed | tf_op | source)
XLA Modules:
  0.0 149.0 jit_solution(5977504370377497365)
XLA Ops:
  0.6 0.0 copy-start.5
  0.6 0.0 copy-start
  0.7 0.0 copy-start.1
  0.7 0.0 copy-start.2
  0.7 0.0 copy-start.3
  0.8 1.0 copy.11
  1.7 0.9 copy.12
  2.7 3.8 %collective-permute-start.4 = (bf16[2,2,32,128]{3,2,1,0:T(8,128)(2,1)S(1)}, bf16[2,2,32,128]{3,2,1,0:T(8,128)(2,1)S(1)}, u32[]{:S(2)}, u32[]{:S(2)}) collective-permute-start(bf16[2,2,32,128]{3,2,1,0:T(8,128)(2,1)S(1)} %get-tuple-element.25), channel_id=1, source_target_pairs={{0,64},{1,65},{4,68},{5,69},{8,72},{9,73},{12,76},{13,77},{2,66},{... | collective-permute-start | bytes 98312 | tf_op jit(solution)/shard_map/ppermute | solution.py:31
  6.5 0.4 collective-permute-start.2
  6.9 2.3 %collective-permute-start.3 = (bf16[2,2,32,128]{3,2,1,0:T(8,128)(2,1)S(1)}, bf16[2,2,32,128]{3,2,1,0:T(8,128)(2,1)S(1)}, u32[]{:S(2)}, u32[]{:S(2)}) collective-permute-start(bf16[2,2,32,128]{3,2,1,0:T(8,128)(2,1)S(1)} %get-tuple-element.26), channel_id=1, source_target_pairs={{0,96},{1,97},{4,100},{5,101},{8,104},{9,105},{12,108},{13,109},{2... | collective-permute-start | bytes 98312 | tf_op jit(solution)/shard_map/ppermute | solution.py:31
  9.2 0.0 collective-permute-done.4
  9.2 1.3 collective-permute-done.2
  10.5 0.0 collective-permute-done.3
  10.5 1.7 %collective-permute-start.5 = (bf16[4,2,32,128]{3,2,1,0:T(8,128)(2,1)S(1)}, bf16[4,2,32,128]{3,2,1,0:T(8,128)(2,1)S(1)}, u32[]{:S(2)}, u32[]{:S(2)}) collective-permute-start(bf16[4,2,32,128]{3,2,1,0:T(8,128)(2,1)S(1)} %get-tuple-element.23), channel_id=1, source_target_pairs={{0,2},{1,3},{4,6},{5,7},{8,10},{9,11},{12,14},{13,15},{2,16},{3,17... | collective-permute-start | bytes 196616 | tf_op jit(solution)/shard_map/ppermute | solution.py:31
  12.2 2.2 %collective-permute-start.6 = (bf16[4,2,32,128]{3,2,1,0:T(8,128)(2,1)S(1)}, bf16[4,2,32,128]{3,2,1,0:T(8,128)(2,1)S(1)}, u32[]{:S(2)}, u32[]{:S(2)}) collective-permute-start(bf16[4,2,32,128]{3,2,1,0:T(8,128)(2,1)S(1)} %get-tuple-element.22), channel_id=1, source_target_pairs={{0,18},{1,19},{4,22},{5,23},{8,26},{9,27},{12,30},{13,31},{2,0},{3... | collective-permute-start | bytes 196616 | tf_op jit(solution)/shard_map/ppermute | solution.py:31
  14.4 1.2 collective-permute-start.7
  15.7 0.0 copy-done.5
  15.7 0.7 collective-permute-start
  16.4 7.3 %collective-permute-start.1 = (bf16[256,512]{1,0:T(8,128)(2,1)S(1)}, bf16[256,512]{1,0:T(8,128)(2,1)S(1)}, u32[]{:S(2)}, u32[]{:S(2)}) collective-permute-start(bf16[256,512]{1,0:T(8,128)(2,1)S(1)} %get-tuple-element.18), channel_id=1, source_target_pairs={{0,14},{1,15},{4,34},{5,35},{8,70},{9,71},{12,106},{13,107},{2,30}... | collective-permute-start | bytes 786440 | tf_op jit(solution)/shard_map/ppermute | solution.py:31
  24.4 0.0 collective-permute-done.5
  24.4 0.0 collective-permute-done.6
  24.4 0.0 collective-permute-done.7
  24.5 0.1 collective-permute-start.9
  24.5 2.7 %collective-permute-start.10 = (bf16[16,2,32,128]{3,2,1,0:T(8,128)(2,1)S(1)}, bf16[16,2,32,128]{3,2,1,0:T(8,128)(2,1)S(1)}, u32[]{:S(2)}, u32[]{:S(2)}) collective-permute-start(bf16[16,2,32,128]{3,2,1,0:T(8,128)(2,1)S(1)} %pad_maximum_fusion.1.refs_0_.refs_3_.refs_10_), channel_id=1, source_target_pairs={{0,12},{1,13},{4,0},{5,1},{8,4},{9,5},{12,8},{13,9},{2,14},{3,15},... | collective-permute-start | bytes 786440 | tf_op jit(solution)/shard_map/ppermute | solution.py:31
  27.2 0.1 pad_add_fusion.place_ref
  27.3 0.0 copy-done
  27.3 0.0 copy-done.1
  27.3 0.0 copy-done.2
  27.3 0.0 copy-done.3
  27.3 5.1 %own_keys.1 = (f32[8,128,512]{2,1,0:T(8,128)S(1)}, f32[8,8,512]{2,1,0:T(8,128)S(1)}) custom-call(s32[1,8]{1,0:T(1,128)S(1)} %copy-done.3, s32[1]{0:T(128)S(6)} %copy.15.len_ref.refs_1_, bf16[512,1024]{1,0:T(8,128)(2,1)S(1)} %bitcast.34, bf16[512,128]{1,0:T(8,128)(2,1)S(1)} %bitcast.39, bf16[512,128]{1,0:T(8,128)(2,1)S(1)} %bitcast.41), custom_call_target="tpu_custom_call" | custom-call | flops 2147483648 | bytes 6291456 | tf_op jit(solution)/shard_map/own_keys/pallas_call | solution.py:327
  32.4 4.2 %collective-permute-start.8 = (bf16[16,2,32,128]{3,2,1,0:T(8,128)(2,1)S(1)}, bf16[16,2,32,128]{3,2,1,0:T(8,128)(2,1)S(1)}, u32[]{:S(2)}, u32[]{:S(2)}) collective-permute-start(bf16[16,2,32,128]{3,2,1,0:T(8,128)(2,1)S(1)} %pad_maximum_fusion.1.refs_0_.refs_3_.refs_10_), channel_id=1, source_target_pairs={{0,1},{1,0},{4,5},{5,4},{8,9},{9,8},{12,13},{13,12},{2,3},{3,2},{6... | collective-permute-start | bytes 786440 | tf_op jit(solution)/shard_map/ppermute | solution.py:31
  36.6 0.0 collective-permute-done.9
  36.6 0.1 collective-permute-start.12
  36.7 0.0 collective-permute-done.10
  36.8 2.7 %collective-permute-start.13 = (bf16[8,2,32,128]{3,2,1,0:T(8,128)(2,1)S(1)}, bf16[8,2,32,128]{3,2,1,0:T(8,128)(2,1)S(1)}, u32[]{:S(2)}, u32[]{:S(2)}) collective-permute-start(bf16[8,2,32,128]{3,2,1,0:T(8,128)(2,1)S(1)} %slice.17), channel_id=1, source_target_pairs={{0,12},{1,13},{4,0},{5,1},{8,4},{9,5},{12,8},{13,9},{2,14},{3,15},... | collective-permute-start | bytes 393224 | tf_op jit(solution)/shard_map/ppermute | solution.py:31
  39.5 3.5 %collective-permute-done.12 = bf16[8,2,32,128]{3,2,1,0:T(8,128)(2,1)S(1)} collective-permute-done((bf16[8,2,32,128]{3,2,1,0:T(8,128)(2,1)S(1)}, bf16[8,2,32,128]{3,2,1,0:T(8,128)(2,1)S(1)}, u32[]{:S(2)}, u32[]{:S(2)}) %collective-permute-start.12) | collective-permute-done | bytes 131104 | tf_op jit(solution)/shard_map/ppermute | solution.py:31
  43.0 0.8 collective-permute-start.11
  43.8 0.0 collective-permute-done.13
  43.9 0.1 collective-permute-start.14
  44.0 0.0 collective-permute-done.8.refs_1_.refs_4_.refs_11_
  44.0 5.4 %here_keys.1 = (f32[8,128,512]{2,1,0:T(8,128)S(1)}, f32[8,8,512]{2,1,0:T(8,128)S(1)}) custom-call(bf16[512,1024]{1,0:T(8,128)(2,1)S(1)} %bitcast.35, f32[8,128,512]{2,1,0:T(8,128)S(1)} %get-tuple-element.12.refs_1_, f32[8,8,512]{2,1,0:T(8,128)S(1)} %get-tuple-element.13.refs_2_, bf16[16,2,32,128]{3,2,1,0:T(8,128)(2,1)S(1)} %pad_maximum_fusion.1.refs_0_.refs_3_.refs_10_, ...), custom_call_target="tpu_custom_call" | custom-call | flops 4294967296 | bytes 6291456 | tf_op jit(solution)/shard_map/here_keys/pallas_call | solution.py:345
  49.4 0.0 copy-start.4
  49.4 1.3 copy-done.4
  50.7 0.0 collective-permute-done.qa_ref
  50.7 0.0 collective-permute-done.1.qb_ref
  50.7 0.0 collective-permute-done.14.refs_5_.refs_6_.refs_15_
  50.8 0.0 collective-permute-done.11.refs_3_.refs_4_.refs_13_
  50.8 17.4 %prompt_rows.1 = (bf16[256,512]{1,0:T(8,128)(2,1)S(1)}, bf16[256,512]{1,0:T(8,128)(2,1)S(1)}) custom-call(s32[4]{0:T(128)S(1)} %pad_add_fusion.place_ref, bf16[256,512]{1,0:T(8,128)(2,1)S(1)} %collective-permute-done.qa_ref, bf16[256,512]{1,0:T(8,128)(2,1)S(1)} %collective-permute-done.1.qb_ref, ...), custom_call_target="tpu_custom_call" | custom-call | flops 4831838208 | bytes 6291456 | tf_op jit(solution)/shard_map/prompt_rows/pallas_call | solution.py:392
  68.2 0.7 collective-permute-start.15
  68.9 12.9 %collective-permute-start.16 = (bf16[256,512]{1,0:T(8,128)(2,1)S(1)}, bf16[256,512]{1,0:T(8,128)(2,1)S(1)}, u32[]{:S(2)}, u32[]{:S(2)}) collective-permute-start(bf16[256,512]{1,0:T(8,128)(2,1)S(1)} %get-tuple-element.11), channel_id=1, source_target_pairs={{14,0},{15,1},{34,4},{35,5},{70,8},{71,9},{106,12},{107,13},{30,2}... | collective-permute-start | bytes 786440 | tf_op jit(solution)/shard_map/ppermute | solution.py:36
  81.8 9.4 %wide_keys.1 = (f32[8,128,512]{2,1,0:T(8,128)S(1)}, f32[8,8,512]{2,1,0:T(8,128)S(1)}) custom-call(bf16[512,1024]{1,0:T(8,128)(2,1)S(1)} %bitcast.36, f32[8,128,512]{2,1,0:T(8,128)} %copy-done.4, f32[8,8,512]{2,1,0:T(8,128)S(1)} %get-tuple-element.15.refs_2_, bf16[32,2,32,128]{3,2,1,0:T(8,128)(2,1)S(1)} %constant_dynamic-update-slice_fusion.refs_2_.refs_3_.refs_12_, ...), custom_call_target="tpu_custom_call" | custom-call | flops 8589934592 | bytes 6291456 | tf_op jit(solution)/shard_map/wide_keys/pallas_call | solution.py:345
  91.2 57.0 %last_keys.1 = bf16[512,1024]{1,0:T(8,128)(2,1)} custom-call(s32[1,8]{1,0:T(1,128)S(1)} %copy-done.3, s32[1]{0:T(128)S(6)} %copy.15.len_ref.refs_1_, bf16[512,1024]{1,0:T(8,128)(2,1)S(1)} %bitcast.37, f32[8,128,512]{2,1,0:T(8,128)S(1)} %get-tuple-element.16.refs_3_, f32[8,8,512]{2,1,0:T(8,128)S(1)} %get-tuple-element.17.refs_4_, ...), custom_call_target="tpu_custom_call" | custom-call | flops 4294967296 | bytes 6291456 | tf_op jit(solution)/shard_map/last_keys/pallas_call | solution.py:365
  148.2 0.0 collective-permute-done.15
  148.2 0.0 collective-permute-done.16
  148.2 0.8 pad_maximum_fusion
  (13 shorter events, 0.3 us)
Async XLA Ops:
  0.6 15.0 %copy-start.5 = (bf16[512,512]{1,0:T(8,128)(2,1)S(1)}, bf16[512,512]{1,0:T(8,128)(2,1)}, u32[]{:S(2)}) copy-start(bf16[512,512]{1,0:T(8,128)(2,1)} %param.8) | copy-start | bytes 1572868
  0.6 26.6 %copy-start = (bf16[1,512,1024]{2,1,0:T(8,128)(2,1)S(1)}, bf16[1,512,1024]{2,1,0:T(8,128)(2,1)}, u32[]{:S(2)}) copy-start(bf16[1,512,1024]{2,1,0:T(8,128)(2,1)} %param.11) | copy-start | bytes 3145732
  0.7 26.6 %copy-start.1 = (bf16[1,512,128]{2,1,0:T(8,128)(2,1)S(1)}, bf16[1,512,128]{2,1,0:T(8,128)(2,1)}, u32[]{:S(2)}) copy-start(bf16[1,512,128]{2,1,0:T(8,128)(2,1)} %param.12) | copy-start | bytes 393220
  0.7 26.6 %copy-start.2 = (bf16[1,512,128]{2,1,0:T(8,128)(2,1)S(1)}, bf16[1,512,128]{2,1,0:T(8,128)(2,1)}, u32[]{:S(2)}) copy-start(bf16[1,512,128]{2,1,0:T(8,128)(2,1)} %param.13) | copy-start | bytes 393220
  0.7 26.6 %copy-start.3 = (s32[1,8]{1,0:T(1,128)S(1)}, s32[1,8]{1,0:T(1,128)}, u32[]{:S(2)}) copy-start(s32[1,8]{1,0:T(1,128)} %refs_0_.1) | copy-start | bytes 100
  2.7 6.5 %collective-permute-start.4 = (bf16[2,2,32,128]{3,2,1,0:T(8,128)(2,1)S(1)}, bf16[2,2,32,128]{3,2,1,0:T(8,128)(2,1)S(1)}, u32[]{:S(2)}, u32[]{:S(2)}) collective-permute-start(bf16[2,2,32,128]{3,2,1,0:T(8,128)(2,1)S(1)} %get-tuple-element.25), channel_id=1, source_target_pairs={{0,64},{1,65},{4,68},{5,69},{8,72},{9,73},{12,76},{13,77},{2,66},{... | collective-permute-start | bytes 98312 | tf_op jit(solution)/shard_map/ppermute | solution.py:31
  6.5 4.0 %collective-permute-start.2 = (bf16[2,2,32,128]{3,2,1,0:T(8,128)(2,1)S(1)}, bf16[2,2,32,128]{3,2,1,0:T(8,128)(2,1)S(1)}, u32[]{:S(2)}, u32[]{:S(2)}) collective-permute-start(bf16[2,2,32,128]{3,2,1,0:T(8,128)(2,1)S(1)} %get-tuple-element.27), channel_id=1, source_target_pairs={{0,32},{1,33},{4,36},{5,37},{8,40},{9,41},{12,44},{13,45},{2,34},{... | collective-permute-start | bytes 98312 | tf_op jit(solution)/shard_map/ppermute | solution.py:31
  6.9 3.6 %collective-permute-start.3 = (bf16[2,2,32,128]{3,2,1,0:T(8,128)(2,1)S(1)}, bf16[2,2,32,128]{3,2,1,0:T(8,128)(2,1)S(1)}, u32[]{:S(2)}, u32[]{:S(2)}) collective-permute-start(bf16[2,2,32,128]{3,2,1,0:T(8,128)(2,1)S(1)} %get-tuple-element.26), channel_id=1, source_target_pairs={{0,96},{1,97},{4,100},{5,101},{8,104},{9,105},{12,108},{13,109},{2... | collective-permute-start | bytes 98312 | tf_op jit(solution)/shard_map/ppermute | solution.py:31
  10.5 13.8 %collective-permute-start.5 = (bf16[4,2,32,128]{3,2,1,0:T(8,128)(2,1)S(1)}, bf16[4,2,32,128]{3,2,1,0:T(8,128)(2,1)S(1)}, u32[]{:S(2)}, u32[]{:S(2)}) collective-permute-start(bf16[4,2,32,128]{3,2,1,0:T(8,128)(2,1)S(1)} %get-tuple-element.23), channel_id=1, source_target_pairs={{0,2},{1,3},{4,6},{5,7},{8,10},{9,11},{12,14},{13,15},{2,16},{3,17... | collective-permute-start | bytes 196616 | tf_op jit(solution)/shard_map/ppermute | solution.py:31
  12.2 12.1 %collective-permute-start.6 = (bf16[4,2,32,128]{3,2,1,0:T(8,128)(2,1)S(1)}, bf16[4,2,32,128]{3,2,1,0:T(8,128)(2,1)S(1)}, u32[]{:S(2)}, u32[]{:S(2)}) collective-permute-start(bf16[4,2,32,128]{3,2,1,0:T(8,128)(2,1)S(1)} %get-tuple-element.22), channel_id=1, source_target_pairs={{0,18},{1,19},{4,22},{5,23},{8,26},{9,27},{12,30},{13,31},{2,0},{3... | collective-permute-start | bytes 196616 | tf_op jit(solution)/shard_map/ppermute | solution.py:31
  14.4 9.9 %collective-permute-start.7 = (bf16[4,2,32,128]{3,2,1,0:T(8,128)(2,1)S(1)}, bf16[4,2,32,128]{3,2,1,0:T(8,128)(2,1)S(1)}, u32[]{:S(2)}, u32[]{:S(2)}) collective-permute-start(bf16[4,2,32,128]{3,2,1,0:T(8,128)(2,1)S(1)} %get-tuple-element.21), channel_id=1, source_target_pairs={{0,16},{1,17},{4,20},{5,21},{8,24},{9,25},{12,28},{13,29},{2,18},{... | collective-permute-start | bytes 196616 | tf_op jit(solution)/shard_map/ppermute | solution.py:31
  15.7 35.0 %collective-permute-start = (bf16[256,512]{1,0:T(8,128)(2,1)S(1)}, bf16[256,512]{1,0:T(8,128)(2,1)S(1)}, u32[]{:S(2)}, u32[]{:S(2)}) collective-permute-start(bf16[256,512]{1,0:T(8,128)(2,1)S(1)} %get-tuple-element.19), channel_id=1, source_target_pairs={{0,0},{1,1},{4,36},{5,37},{8,72},{9,73},{12,108},{13,109},{2,16},{... | collective-permute-start | bytes 786440 | tf_op jit(solution)/shard_map/ppermute | solution.py:31
  16.4 34.3 %collective-permute-start.1 = (bf16[256,512]{1,0:T(8,128)(2,1)S(1)}, bf16[256,512]{1,0:T(8,128)(2,1)S(1)}, u32[]{:S(2)}, u32[]{:S(2)}) collective-permute-start(bf16[256,512]{1,0:T(8,128)(2,1)S(1)} %get-tuple-element.18), channel_id=1, source_target_pairs={{0,14},{1,15},{4,34},{5,35},{8,70},{9,71},{12,106},{13,107},{2,30}... | collective-permute-start | bytes 786440 | tf_op jit(solution)/shard_map/ppermute | solution.py:31
  24.5 12.2 %collective-permute-start.9 = (bf16[16,2,32,128]{3,2,1,0:T(8,128)(2,1)S(1)}, bf16[16,2,32,128]{3,2,1,0:T(8,128)(2,1)S(1)}, u32[]{:S(2)}, u32[]{:S(2)}) collective-permute-start(bf16[16,2,32,128]{3,2,1,0:T(8,128)(2,1)S(1)} %pad_maximum_fusion.1.refs_0_.refs_3_.refs_10_), channel_id=1, source_target_pairs={{0,4},{1,5},{4,8},{5,9},{8,12},{9,13},{12,0},{13,1},{2,6},{3,7},{6... | collective-permute-start | bytes 786440 | tf_op jit(solution)/shard_map/ppermute | solution.py:31
  24.5 12.2 %collective-permute-start.10 = (bf16[16,2,32,128]{3,2,1,0:T(8,128)(2,1)S(1)}, bf16[16,2,32,128]{3,2,1,0:T(8,128)(2,1)S(1)}, u32[]{:S(2)}, u32[]{:S(2)}) collective-permute-start(bf16[16,2,32,128]{3,2,1,0:T(8,128)(2,1)S(1)} %pad_maximum_fusion.1.refs_0_.refs_3_.refs_10_), channel_id=1, source_target_pairs={{0,12},{1,13},{4,0},{5,1},{8,4},{9,5},{12,8},{13,9},{2,14},{3,15},... | collective-permute-start | bytes 786440 | tf_op jit(solution)/shard_map/ppermute | solution.py:31
  32.4 11.5 %collective-permute-start.8 = (bf16[16,2,32,128]{3,2,1,0:T(8,128)(2,1)S(1)}, bf16[16,2,32,128]{3,2,1,0:T(8,128)(2,1)S(1)}, u32[]{:S(2)}, u32[]{:S(2)}) collective-permute-start(bf16[16,2,32,128]{3,2,1,0:T(8,128)(2,1)S(1)} %pad_maximum_fusion.1.refs_0_.refs_3_.refs_10_), channel_id=1, source_target_pairs={{0,1},{1,0},{4,5},{5,4},{8,9},{9,8},{12,13},{13,12},{2,3},{3,2},{6... | collective-permute-start | bytes 786440 | tf_op jit(solution)/shard_map/ppermute | solution.py:31
  36.6 6.4 %collective-permute-start.12 = (bf16[8,2,32,128]{3,2,1,0:T(8,128)(2,1)S(1)}, bf16[8,2,32,128]{3,2,1,0:T(8,128)(2,1)S(1)}, u32[]{:S(2)}, u32[]{:S(2)}) collective-permute-start(bf16[8,2,32,128]{3,2,1,0:T(8,128)(2,1)S(1)} %slice.16), channel_id=1, source_target_pairs={{0,4},{1,5},{4,8},{5,9},{8,12},{9,13},{12,0},{13,1},{2,6},{3,7},{6... | collective-permute-start | bytes 393224 | tf_op jit(solution)/shard_map/ppermute | solution.py:31
  36.8 7.1 %collective-permute-start.13 = (bf16[8,2,32,128]{3,2,1,0:T(8,128)(2,1)S(1)}, bf16[8,2,32,128]{3,2,1,0:T(8,128)(2,1)S(1)}, u32[]{:S(2)}, u32[]{:S(2)}) collective-permute-start(bf16[8,2,32,128]{3,2,1,0:T(8,128)(2,1)S(1)} %slice.17), channel_id=1, source_target_pairs={{0,12},{1,13},{4,0},{5,1},{8,4},{9,5},{12,8},{13,9},{2,14},{3,15},... | collective-permute-start | bytes 393224 | tf_op jit(solution)/shard_map/ppermute | solution.py:31
  43.0 7.7 %collective-permute-start.11 = (bf16[32,2,32,128]{3,2,1,0:T(8,128)(2,1)S(1)}, bf16[32,2,32,128]{3,2,1,0:T(8,128)(2,1)S(1)}, u32[]{:S(2)}, u32[]{:S(2)}) collective-permute-start(bf16[32,2,32,128]{3,2,1,0:T(8,128)(2,1)S(1)} %constant_dynamic-update-slice_fusion.refs_2_.refs_3_.refs_12_), channel_id=1, source_target_pairs={{0,1},{1,0},{4,5},{5,4},{8,9},{9,8},{12,13},{13,12},{2,3},{3,2},{6... | collective-permute-start | bytes 1572872 | tf_op jit(solution)/shard_map/ppermute | solution.py:31
  43.9 6.9 %collective-permute-start.14 = (bf16[16,2,32,128]{3,2,1,0:T(8,128)(2,1)S(1)}, bf16[16,2,32,128]{3,2,1,0:T(8,128)(2,1)S(1)}, u32[]{:S(2)}, u32[]{:S(2)}) collective-permute-start(bf16[16,2,32,128]{3,2,1,0:T(8,128)(2,1)S(1)} %constant_dynamic-update-slice_fusion.2.refs_4_.refs_5_.refs_14_), channel_id=1, source_target_pairs={{0,1},{1,0},{4,5},{5,4},{8,9},{9,8},{12,13},{13,12},{2,3},{3,2},{6... | collective-permute-start | bytes 786440 | tf_op jit(solution)/shard_map/ppermute | solution.py:31
  49.4 1.3 copy-start.4
  68.2 80.0 %collective-permute-start.15 = (bf16[256,512]{1,0:T(8,128)(2,1)S(1)}, bf16[256,512]{1,0:T(8,128)(2,1)S(1)}, u32[]{:S(2)}, u32[]{:S(2)}) collective-permute-start(bf16[256,512]{1,0:T(8,128)(2,1)S(1)} %get-tuple-element.10), channel_id=1, source_target_pairs={{0,0},{1,1},{36,4},{37,5},{72,8},{73,9},{108,12},{109,13},{16,2},{... | collective-permute-start | bytes 786440 | tf_op jit(solution)/shard_map/ppermute | solution.py:36
  68.9 79.3 %collective-permute-start.16 = (bf16[256,512]{1,0:T(8,128)(2,1)S(1)}, bf16[256,512]{1,0:T(8,128)(2,1)S(1)}, u32[]{:S(2)}, u32[]{:S(2)}) collective-permute-start(bf16[256,512]{1,0:T(8,128)(2,1)S(1)} %get-tuple-element.11), channel_id=1, source_target_pairs={{14,0},{15,1},{34,4},{35,5},{70,8},{71,9},{106,12},{107,13},{30,2}... | collective-permute-start | bytes 786440 | tf_op jit(solution)/shard_map/ppermute | solution.py:36

commit v2 on v1

v2 whole, which is shorter than its diff:
```python
import functools

import jax
import jax.numpy as jnp
from jax import lax
from jax.experimental import pallas as pl
from jax.experimental.pallas import tpu as pltpu
from jax.sharding import PartitionSpec as P

QH = 64
KVH = 8
HD = 128
RBLK = 8
ROWS = 512
SUB = 32
GROUP = QH // KVH
STEP_HEADS = 4
SCALE = HD**-0.5 * 1.4426950408889634
LOW, HIGH = 1e-18, 1e30
AXES = ("chain", "resp")
STEPS = (0, 1, 3, 2)
MIB = 2**20
PLACES = [(y, z, x, k) for y in range(4) for z in range(4) for x in range(4) for k in range(2)]


def device_at(y, z, x, core):
    return (y * 2 + z // 2) * 16 + (x * 2 + z % 2) * 2 + core


def move(block, target):
    route = [(device_at(*p), device_at(*target(*p))) for p in PLACES]
    return lax.ppermute(block, AXES, route)


def along_y(d):
    return lambda y, z, x, core: ((y + d) % 4, z, x, core)


def along_z(d):
    return lambda y, z, x, core: (y, (z + d) % 4, x, core)


def other_core(y, z, x, core):
    return (y, z, x, 1 - core)


def along_x(d):
    return lambda y, z, x, core: (y, z, (x + d) % 4, core)


def both_ways_x(y, z, x, core):
    return (y, z, (x + 1 + 2 * core) % 4, core)


def both_ways_y(y, z, x, core):
    return ((y + 1 + 2 * core) % 4, z, x, core)


def dot_t(a, b):
    return lax.dot_general(a, b, (((1,), (1,)), ((), ())), preferred_element_type=jnp.float32)


def fold_rows(p):
    return jnp.sum(p.reshape(p.shape[0] // 8, 8, p.shape[1]), axis=0)


def token_rows(block):
    return block.reshape(-1, HD)


def online(carried, keys, values_t, queries, visible):
    run_max, run_sum, run_acc = carried
    scores = dot_t(keys, queries) * SCALE
    if visible is not None:
        scores = jnp.where(visible, scores, -1e30)
    new_max = jnp.maximum(run_max, jnp.max(scores, axis=0, keepdims=True))
    weights = jnp.exp2(scores - new_max)
    if visible is not None:
        weights = jnp.where(visible, weights, 0.0)
    rescale = jnp.exp2(run_max - new_max)
    run_sum = run_sum * rescale + jnp.sum(weights, axis=0, keepdims=True)
    added = jnp.dot(values_t, weights.astype(jnp.bfloat16), preferred_element_type=jnp.float32)
    return (new_max, run_sum, run_acc * rescale + added)


def fresh(cols):
    return (
        jnp.full((1, cols), -1e30, jnp.float32),
        jnp.zeros((1, cols), jnp.float32),
        jnp.zeros((HD, cols), jnp.float32),
    )


def tree_seen(tree_ref, len_ref):
    lines = []
    for j in range(RBLK):
        parent = tree_ref[0, j]
        line = jnp.int32(1 << j)
        for i in range(j):
            line = line | jnp.where(parent == i, lines[i], 0)
        lines.append(line)
    key_at = lax.broadcasted_iota(jnp.int32, (ROWS, ROWS), 0)
    row_at = lax.broadcasted_iota(jnp.int32, (ROWS, ROWS), 1)
    span = ROWS // RBLK
    line_of_row = jnp.zeros((ROWS, ROWS), jnp.int32)
    for j in range(RBLK):
        line_of_row = jnp.where(row_at // span == j, lines[j], line_of_row)
    related = (lax.shift_right_logical(line_of_row, key_at // span) & 1) == 1
    return related & (key_at <= row_at) & (key_at < len_ref[0])


def load_chunks(parts, kb, vt):
    at = 0
    for part in parts:
        keys, values = token_rows(part[:, 0]), token_rows(part[:, 1])
        count = keys.shape[0]
        kb[at : at + count, :] = keys
        vt[:, at : at + count] = values.T
        at += count


def weigh(keys, queries, values_t, shown=None):
    scores = dot_t(keys, queries) * SCALE
    weights = jnp.exp2(scores if shown is None else scores + shown)
    added = jnp.dot(values_t, weights.astype(jnp.bfloat16), preferred_element_type=jnp.float32)
    return fold_rows(weights), added


def first_kernel(part_count, tree_ref, len_ref, q_ref, k_own, v_own, *refs):
    parts = refs[:part_count]
    acc_ref, sum_ref, kb, vt, vt_own, seen = refs[part_count:]

    @pl.when(pl.program_id(0) == 0)
    def _():
        load_chunks(parts, kb, vt)
        vt_own[...] = v_own[...].T
        seen[...] = jnp.where(tree_seen(tree_ref, len_ref), 0.0, -jnp.inf)

    for h in range(STEP_HEADS):
        queries = q_ref[:, h * HD : (h + 1) * HD]
        sums, accs = weigh(kb[...], queries, vt[...])
        own_sums, own_accs = weigh(k_own[...], queries, vt_own[...], seen[...])
        sum_ref[h] = sums + own_sums
        acc_ref[h] = accs + own_accs


def chunk_kernel(part_count, q_ref, acc_in, sum_in, *refs):
    parts = refs[:part_count]
    acc_ref, sum_ref, kb, vt = refs[part_count:]

    @pl.when(pl.program_id(0) == 0)
    def _():
        load_chunks(parts, kb, vt)

    for h in range(STEP_HEADS):
        sums, accs = weigh(kb[...], q_ref[:, h * HD : (h + 1) * HD], vt[...])
        sum_ref[h] = sum_in[h] + sums
        acc_ref[h] = acc_in[h] + accs


def last_kernel(part_count, slabs, *refs):
    tree_ref, len_ref, q_ref, acc_in, sum_in = refs[:5]
    parts = refs[5 : 5 + part_count]
    refs = refs[5 + part_count :]
    q_all, k_own, v_own, held = refs[0], refs[1], refs[2], refs[3 : 3 + len(slabs)]
    out_ref, kb, vt, low, high, slab, q_buf, own_buf = refs[3 + len(slabs) :]
    step = pl.program_id(0)

    @pl.when(step == 0)
    def _():
        load_chunks(parts, kb, vt)
        low[...] = jnp.full_like(low, 1.0)
        high[...] = jnp.full_like(high, 1.0)

    live = lax.broadcasted_iota(jnp.int32, (ROWS, HD), 0) < len_ref[0]
    for h in range(STEP_HEADS):
        sums, accs = weigh(kb[...], q_ref[:, h * HD : (h + 1) * HD], vt[...])
        total = jnp.sum(sum_in[h] + sums, axis=0, keepdims=True)
        low[...] = jnp.minimum(low[...], total)
        high[...] = jnp.maximum(high[...], total)
        shown = ((acc_in[h] + accs) / total).T
        cols = pl.ds(pl.multiple_of((step * STEP_HEADS + h) * HD, HD), HD)
        out_ref[:, cols] = jnp.where(live, shown, 0.0).astype(jnp.bfloat16)

    @pl.when(step == pl.num_programs(0) - 1)
    def _():
        good = (jnp.min(low[...]) > LOW) & (jnp.max(high[...]) < HIGH)

        @pl.when(jnp.logical_not(good))
        def _():
            pltpu.sync_copy(k_own, own_buf.at[0])
            pltpu.sync_copy(v_own, own_buf.at[1])

            def one_head(h, unused):
                at = pl.multiple_of(h * HD, HD)
                pltpu.sync_copy(q_all.at[:, pl.ds(at, HD)], q_buf)
                queries = q_buf[...]
                carried = fresh(ROWS)
                for ref, starts in zip(held, slabs):
                    for start in starts:
                        pltpu.sync_copy(ref.at[pl.ds(start, 16)], slab)
                        carried = online(
                            carried, token_rows(slab[:, 0]), token_rows(slab[:, 1]).T, queries, None
                        )
                visible = tree_seen(tree_ref, len_ref)
                run_max, run_sum, run_acc = online(
                    carried, own_buf[0], own_buf[1].T, queries, visible
                )
                shown = jnp.where(live, (run_acc / run_sum).T, 0.0)
                out_ref[:, pl.ds(at, HD)] = shown.astype(jnp.bfloat16)
                return unused

            lax.fori_loop(0, GROUP, one_head, 0)


def prompt_kernel(place_ref, q_ref, *refs):
    here, here_s, wide, wide_s, far, far_s, out_ref, kb, vb, vt, acc, total, top = refs
    y, z, x, core = (place_ref[i] for i in range(4))
    heads = GROUP // 2
    pair = 2 * ROWS
    for ref, core_from in ((here, core), (here_s, 1 - core)):
        for i, z_step in enumerate(STEPS):
            for j, x_step in enumerate(STEPS):
                x0, z0 = (x - x_step) % 4, (z - z_step) % 4
                at = (z0 // 2) * ROWS + ((x0 * 2 + z0 % 2) * 2 + core_from) * SUB
                spot = pl.ds(pl.multiple_of(at, SUB), SUB)
                kb[0, spot, :] = ref[i * 4 + j, 0]
                vb[spot, :] = ref[i * 4 + j, 1]
    vt[0] = vb[...].T
    others = [(wide,), (wide_s,), (far, far_s)]
    sources = [(y + 3 + 2 * core) % 4, (y + 1 + 2 * core) % 4, (y + 2) % 4]

    def queries(h):
        return q_ref[:, h * HD : (h + 1) * HD]

    key_at = lax.broadcasted_iota(jnp.int32, (pair, ROWS), 0)
    row_at = lax.broadcasted_iota(jnp.int32, (pair, ROWS), 1) + z // 2 * ROWS
    visible = key_at <= row_at
    hidden = jnp.where(visible, 0.0, -jnp.inf)
    for h in range(heads):
        total[h], acc[h] = weigh(kb[0], queries(h), vt[0], hidden)
    for i, (parts, y_from) in enumerate(zip(others, sources)):

        @pl.when(y_from < y)
        def _(i=i, parts=parts):
            load_chunks(parts, kb.at[i + 1], vt.at[i + 1])
            for h in range(heads):
                sums, accs = weigh(kb[i + 1], queries(h), vt[i + 1])
                total[h] += sums
                acc[h] += accs

    def store(h, sums):
        out_ref[:, h * HD : (h + 1) * HD] = (acc[h] / sums).T.astype(jnp.bfloat16)

    least = most = jnp.ones((1, ROWS), jnp.float32)
    for h in range(heads):
        sums = jnp.sum(total[h], axis=0, keepdims=True)
        store(h, sums)
        least, most = jnp.minimum(least, sums), jnp.maximum(most, sums)
    good = (jnp.min(least) > LOW) & (jnp.max(most) < HIGH)

    @pl.when(jnp.logical_not(good))
    def _():
        for h in range(heads):
            carried = online(fresh(ROWS), kb[0], vt[0], queries(h), visible)
            top[...], total[h, 0:1], acc[h] = carried
            for i, y_from in enumerate(sources):

                @pl.when(y_from < y)
                def _(h=h, i=i):
                    carried = (top[...], total[h, 0:1], acc[h])
                    carried = online(carried, kb[i + 1], vt[i + 1], queries(h), None)
                    top[...], total[h, 0:1], acc[h] = carried

            store(h, total[h, 0:1])


def whole(shape):
    return pl.BlockSpec(shape, lambda h: (0,) * len(shape))


STATE = (
    jax.ShapeDtypeStruct((GROUP, HD, ROWS), jnp.float32),
    jax.ShapeDtypeStruct((GROUP, 8, ROWS), jnp.float32),
)
STATE_SPECS = (
    pl.BlockSpec((STEP_HEADS, HD, ROWS), lambda h: (h, 0, 0)),
    pl.BlockSpec((STEP_HEADS, 8, ROWS), lambda h: (h, 0, 0)),
)
HEAD_SPEC = pl.BlockSpec((ROWS, STEP_HEADS * HD), lambda h: (0, h))
SCALAR = pl.BlockSpec(memory_space=pltpu.SMEM)
PARAMS = dict(compiler_params=pltpu.CompilerParams(vmem_limit_bytes=48 * MIB))


def cost(rows, keys):
    return pl.CostEstimate(
        flops=8 * rows * keys * HD, bytes_accessed=6 * MIB, transcendentals=rows * keys
    )


def attend_first(tree, length, q, k_own, v_own, parts):
    tokens = sum(part.shape[0] for part in parts) * SUB
    return pl.pallas_call(
        functools.partial(first_kernel, len(parts)),
        grid=(GROUP // STEP_HEADS,),
        in_specs=[SCALAR, SCALAR, HEAD_SPEC, whole(k_own.shape), whole(v_own.shape)]
        + [whole(part.shape) for part in parts],
        out_specs=STATE_SPECS,
        out_shape=STATE,
        scratch_shapes=[
            pltpu.VMEM((tokens, HD), jnp.bfloat16),
            pltpu.VMEM((HD, tokens), jnp.bfloat16),
            pltpu.VMEM((HD, ROWS), jnp.bfloat16),
            pltpu.VMEM((ROWS, ROWS), jnp.float32),
        ],
        cost_estimate=cost(GROUP * ROWS, tokens + ROWS),
        name="first_keys",
        **PARAMS,
    )(tree, length, q, k_own, v_own, *parts)


def attend_chunk(q, state, parts, name):
    tokens = sum(part.shape[0] for part in parts) * SUB
    return pl.pallas_call(
        functools.partial(chunk_kernel, len(parts)),
        grid=(GROUP // STEP_HEADS,),
        in_specs=[HEAD_SPEC, *STATE_SPECS] + [whole(part.shape) for part in parts],
        out_specs=STATE_SPECS,
        out_shape=STATE,
        scratch_shapes=[
            pltpu.VMEM((tokens, HD), jnp.bfloat16),
            pltpu.VMEM((HD, tokens), jnp.bfloat16),
        ],
        cost_estimate=cost(GROUP * ROWS, tokens),
        name=name,
        **PARAMS,
    )(q, *state, *parts)


def attend_last(tree, length, q, state, parts, k_own, v_own, held):
    tokens = sum(part.shape[0] for part in parts) * SUB
    slabs = tuple(tuple(range(0, part.shape[0], 16)) for part in held)
    anywhere = pl.BlockSpec(memory_space=pl.ANY)
    return pl.pallas_call(
        functools.partial(last_kernel, len(parts), slabs),
        grid=(GROUP // STEP_HEADS,),
        in_specs=[SCALAR, SCALAR, HEAD_SPEC, *STATE_SPECS]
        + [whole(part.shape) for part in parts]
        + [anywhere] * (3 + len(held)),
        out_specs=whole((ROWS, GROUP * HD)),
        out_shape=jax.ShapeDtypeStruct((ROWS, GROUP * HD), jnp.bfloat16),
        scratch_shapes=[
            pltpu.VMEM((tokens, HD), jnp.bfloat16),
            pltpu.VMEM((HD, tokens), jnp.bfloat16),
            pltpu.VMEM((1, ROWS), jnp.float32),
            pltpu.VMEM((1, ROWS), jnp.float32),
            pltpu.VMEM((16, 2, SUB, HD), jnp.bfloat16),
            pltpu.VMEM((ROWS, HD), jnp.bfloat16),
            pltpu.VMEM((2, ROWS, HD), jnp.bfloat16),
        ],
        cost_estimate=cost(GROUP * ROWS, tokens),
        name="last_keys",
        **PARAMS,
    )(tree, length, q, *state, *parts, q, k_own, v_own, *held)


def attend_prompt(place, q, parts):
    vmem = pl.BlockSpec(memory_space=pltpu.VMEM)
    heads, pair = GROUP // 2, 2 * ROWS
    return pl.pallas_call(
        prompt_kernel,
        in_specs=[SCALAR] + [vmem] * (1 + len(parts)),
        out_specs=vmem,
        out_shape=jax.ShapeDtypeStruct(q.shape, jnp.bfloat16),
        scratch_shapes=[
            pltpu.VMEM((4, pair, HD), jnp.bfloat16),
            pltpu.VMEM((pair, HD), jnp.bfloat16),
            pltpu.VMEM((4, HD, pair), jnp.bfloat16),
            pltpu.VMEM((heads, HD, ROWS), jnp.float32),
            pltpu.VMEM((heads, 8, ROWS), jnp.float32),
            pltpu.VMEM((1, ROWS), jnp.float32),
        ],
        cost_estimate=cost(heads * ROWS, 4 * pair),
        name="prompt_rows",
        **PARAMS,
    )(place, q, *parts)


def after(value, *events):
    return lax.optimization_barrier((value, *events))[0]


def on_device(q_prompt, k_prompt, v_prompt, q_resp, k_resp, v_resp, tree_table, lengths):
    chain, resp = lax.axis_index("chain"), lax.axis_index("resp")
    y, z, x, core = chain // 2, chain % 2 * 2 + resp // 2 % 2, resp // 4, resp % 2
    place = jnp.stack([y, z, x, core]).astype(jnp.int32)
    q = q_resp[0]

    def cols(block, at, count):
        return lax.dynamic_slice_in_dim(block, at * count * HD, count * HD, block.ndim - 1)

    tokens = jnp.stack([k_prompt, v_prompt])
    over_y, over_x = [cols(tokens, y, 2)], [cols(tokens, x, 2)]
    for d in STEPS[1:]:
        over_y.append(move(cols(tokens, (y + d) % 4, 2), along_y(d)))
        over_x.append(move(cols(tokens, (x + d) % 4, 2), along_x(d)))
    over_y, over_x = jnp.stack(over_y), jnp.stack(over_x)

    def for_z(at):
        return jnp.stack([cols(over_y, at // 2, 1), cols(over_x, at % 2, 1)])

    over_z = [for_z(z)] + [move(for_z((z + d) % 4), along_z(d)) for d in STEPS[1:]]
    here = jnp.concatenate(over_z, 1)
    here_s = move(here, other_core)
    r_here, p_here, r_here_s, p_here_s = here[0], here[1], here_s[0], here_s[1]
    r_wide = move(jnp.concatenate([r_here, r_here_s]), both_ways_x)
    p_wide = move(jnp.concatenate([p_here, p_here_s]), both_ways_y)

    state = attend_first(tree_table, lengths, q, k_resp[0], v_resp[0], (r_here, r_here_s))
    r_wide, p_wide = after((r_wide, p_wide), state[1])
    r_far, p_far = move(r_wide[:16], both_ways_x), move(p_wide[:16], both_ways_y)
    r_wide_s, p_wide_s = move(r_wide, other_core), move(p_wide, other_core)
    state = attend_chunk(q, state, (r_wide,), "wide_keys")
    r_far, p_far = after((r_far, p_far), state[1])
    r_far_s, p_far_s = move(r_far, other_core), move(p_far, other_core)
    state = attend_chunk(q, state, (r_wide_s,), "wide_keys_s")
    prompt_out = attend_prompt(
        place, q_prompt, (p_here, p_here_s, p_wide, p_wide_s, p_far, p_far_s)
    )
    held = (r_here, r_here_s, r_wide, r_wide_s, r_far, r_far_s)
    resp_out = attend_last(
        tree_table, lengths, q, state, (r_far, r_far_s), k_resp[0], v_resp[0], held
    )
    return (prompt_out, resp_out[None])


def solution(mesh):
    placed = (
        P("chain", "resp"),
        P(("chain", "resp"), None),
        P(("chain", "resp"), None),
        P("resp", None, "chain"),
        P("resp", None, "chain"),
        P("resp", None, "chain"),
        P("resp", None),
        P("resp"),
    )
    return jax.shard_map(
        on_device,
        mesh=mesh,
        in_specs=placed,
        out_specs=(P("chain", "resp"), P("resp", None, "chain")),
        check_vma=False,
    )
```

time: 149 us -> 170 us (1.14)
  the two profiles are of different devices: /device:TPU:1 before, /device:TPU:25 now
where the time goes in v2:
time: 170 us; the launch traced here: 167 us
  Pallas kernels  129 us (76%)
  starting transfers between devices  22.4 us (13%)
  waiting for transfers between devices  9.04 us (5%)
  local copies, waits for them, and re-layouts  3.2 us (2%)
  other arithmetic  2 us (1%)
  between operations  1.79 us (1%)
    pallas_call x1, Pallas kernels, attend_last(): pl.pallas_call(functools.partial(last_kernel, len(parts), slabs), grid=(G...  70.1 us
    pallas_call x1, Pallas kernels, attend_prompt(): pl.pallas_call(prompt_kernel, in_specs=[SCALAR] + [vmem] * (1 + len(parts...  42 us
    ppermute x18, starting transfers between devices, move(): return lax.ppermute(block, AXES, route)  22.4 us
    pallas_call x2, Pallas kernels, attend_chunk(): pl.pallas_call(functools.partial(chunk_kernel, len(parts)), grid=(GROUP /...  9.38 us
    ppermute x18, waiting for transfers between devices, move(): return lax.ppermute(block, AXES, route)  9.04 us
    pallas_call x1, Pallas kernels, attend_first(): pl.pallas_call(functools.partial(first_kernel, len(parts)), grid=(GROUP /...  7.44 us
  transfers between devices with their start and end apart: 18, of which 6 were waited for; matrix products, arithmetic and copies ran while one was open for 1% of the time, Pallas kernels for 52%

profile of v2, /device:TPU:25, one launch (start us, length us, event | category | flops | bytes accessed | tf_op | source)
XLA Modules:
  0.0 167.4 jit_solution(408519423635663625)
XLA Ops:
  0.7 0.9 fusion.2
  1.7 0.1 collective-permute-start
  1.7 1.5 collective-permute-start.1
  3.2 1.0 collective-permute-start.2
  4.1 0.8 fusion.9
  4.9 2.5 %collective-permute-start.4 = (bf16[2,32,256]{2,1,0:T(8,128)(2,1)S(1)}, bf16[2,32,256]{2,1,0:T(8,128)(2,1)S(1)}, u32[]{:S(2)}, u32[]{:S(2)}) collective-permute-start(bf16[2,32,256]{2,1,0:T(8,128)(2,1)S(1)} %get-tuple-element.40), channel_id=1, source_target_pairs={{0,12},{1,13},{4,0},{5,1},{8,4},{9,5},{12,8},{13,9},{2,14},{3,15},... | collective-permute-start | bytes 98312 | tf_op jit(solution)/shard_map/ppermute | solution.py:32
  7.4 0.5 collective-permute-start.5
  7.9 0.0 collective-permute-done
  7.9 0.6 collective-permute-start.3
  8.5 0.0 collective-permute-done.1
  8.5 0.0 collective-permute-done.2
  8.6 0.0 collective-permute-done.4
  8.6 3.1 %collective-permute-done.5 = bf16[2,32,256]{2,1,0:T(8,128)(2,1)S(1)} collective-permute-done((bf16[2,32,256]{2,1,0:T(8,128)(2,1)S(1)}, bf16[2,32,256]{2,1,0:T(8,128)(2,1)S(1)}, u32[]{:S(2)}, u32[]{:S(2)}) %collective-permute-start.5) | collective-permute-done | bytes 32800 | tf_op jit(solution)/shard_map/ppermute | solution.py:32
  11.7 0.3 collective-permute-done.3
  12.0 0.1 dynamic-slice_bitcast_fusion.6
  12.2 1.7 %collective-permute-start.6 = (bf16[2,4,2,32,128]{4,3,2,1,0:T(8,128)(2,1)S(1)}, bf16[2,4,2,32,128]{4,3,2,1,0:T(8,128)(2,1)S(1)}, u32[]{:S(2)}, u32[]{:S(2)}) collective-permute-start(bf16[2,4,2,32,128]{4,3,2,1,0:T(8,128)(2,1)S(1)} %pad_maximum_fusion.5), channel_id=1, source_target_pairs={{0,2},{1,3},{4,6},{5,7},{8,10},{9,11},{12,14},{13,15},{2,16},{3,17... | collective-permute-start | bytes 393224 | tf_op jit(solution)/shard_map/ppermute | solution.py:32
  13.9 2.2 %collective-permute-start.7 = (bf16[2,4,2,32,128]{4,3,2,1,0:T(8,128)(2,1)S(1)}, bf16[2,4,2,32,128]{4,3,2,1,0:T(8,128)(2,1)S(1)}, u32[]{:S(2)}, u32[]{:S(2)}) collective-permute-start(bf16[2,4,2,32,128]{4,3,2,1,0:T(8,128)(2,1)S(1)} %pad_maximum_fusion.6), channel_id=1, source_target_pairs={{0,18},{1,19},{4,22},{5,23},{8,26},{9,27},{12,30},{13,31},{2,0},{3... | collective-permute-start | bytes 393224 | tf_op jit(solution)/shard_map/ppermute | solution.py:32
  16.1 1.4 collective-permute-start.8
  17.5 0.9 collective-permute-done.6
  18.4 0.0 collective-permute-done.7
  18.4 3.3 %collective-permute-done.8 = bf16[2,4,2,32,128]{4,3,2,1,0:T(8,128)(2,1)S(1)} collective-permute-done((bf16[2,4,2,32,128]{4,3,2,1,0:T(8,128)(2,1)S(1)}, bf16[2,4,2,32,128]{4,3,2,1,0:T(8,128)(2,1)S(1)}, u32[]{:S(2)}, u32[]{:S(2)}) %collective-permute-start.8) | collective-permute-done | bytes 131104 | tf_op jit(solution)/shard_map/ppermute | solution.py:32
  21.7 0.1 pad_maximum_fusion
  21.7 4.5 %collective-permute-start.9 = (bf16[2,16,2,32,128]{4,3,2,1,0:T(8,128)(2,1)S(1)}, bf16[2,16,2,32,128]{4,3,2,1,0:T(8,128)(2,1)S(1)}, u32[]{:S(2)}, u32[]{:S(2)}) collective-permute-start(bf16[2,16,2,32,128]{4,3,2,1,0:T(8,128)(2,1)S(1)} %pad_maximum_fusion), channel_id=1, source_target_pairs={{0,1},{1,0},{4,5},{5,4},{8,9},{9,8},{12,13},{13,12},{2,3},{3,2},{6... | collective-permute-start | bytes 1572872 | tf_op jit(solution)/shard_map/ppermute | solution.py:32
  26.9 0.0 copy-start
  26.9 0.0 copy-start.2
  26.9 0.0 copy-start.3
  26.9 0.0 copy-start.4
  27.0 0.8 collective-permute-done.9
  27.9 0.2 collective-permute-start.10
  28.1 0.8 collective-permute-start.11
  29.0 0.0 copy-done
  29.0 0.0 copy-done.2
  29.0 0.0 copy-done.3
  29.0 0.0 copy-done.4
  29.0 7.4 %first_keys.1 = (f32[8,128,512]{2,1,0:T(8,128)S(1)}, f32[8,8,512]{2,1,0:T(8,128)S(1)}) custom-call(s32[1,8]{1,0:T(1,128)S(1)} %copy-done.4, s32[1]{0:T(128)S(6)} %copy.10.len_ref.refs_1_, bf16[512,1024]{1,0:T(8,128)(2,1)S(1)} %bitcast.44, bf16[512,128]{1,0:T(8,128)(2,1)S(1)} %bitcast.49, bf16[512,128]{1,0:T(8,128)(2,1)S(1)} %bitcast.51, ...), custom_call_target="tpu_custom_call" | custom-call | flops 6442450944 | bytes 6291456 | tf_op jit(solution)/shard_map/first_keys/pallas_call | solution.py:303
  36.4 0.0 copy-start.5
  36.4 1.4 copy-done.5
  37.8 0.0 collective-permute-done.10.refs_0_.refs_12_
  37.8 0.0 collective-permute-done.11.refs_2_
  37.8 1.7 %collective-permute-start.16 = (bf16[32,2,32,128]{3,2,1,0:T(8,128)(2,1)S(1)}, bf16[32,2,32,128]{3,2,1,0:T(8,128)(2,1)}, u32[]{:S(2)}, u32[]{:S(2)}) collective-permute-start(bf16[32,2,32,128]{3,2,1,0:T(8,128)(2,1)S(1)} %collective-permute-done.10.refs_0_.refs_12_), channel_id=1, source_target_pairs={{0,1},{1,0},{4,5},{5,4},{8,9},{9,8},{12,13},{13,12},{2,3},{3,2},{6... | collective-permute-start | bytes 1572872 | tf_op jit(solution)/shard_map/ppermute | solution.py:32
  39.5 0.1 pad_add_fusion.place_ref
  39.6 0.1 collective-permute-start.12
  39.7 3.0 %collective-permute-start.13 = (bf16[16,2,32,128]{3,2,1,0:T(8,128)(2,1)S(1)}, bf16[16,2,32,128]{3,2,1,0:T(8,128)(2,1)S(1)}, u32[]{:S(2)}, u32[]{:S(2)}) collective-permute-start(bf16[16,2,32,128]{3,2,1,0:T(8,128)(2,1)S(1)} %slice.22), channel_id=1, source_target_pairs={{0,4},{1,13},{4,8},{5,1},{8,12},{9,5},{12,0},{13,9},{2,6},{3,15},{... | collective-permute-start | bytes 786440 | tf_op jit(solution)/shard_map/ppermute | solution.py:32
  42.7 0.0 collective-permute-start.14
  42.7 0.0 copy-start.6
  42.7 1.6 copy-done.6
  44.3 4.2 %wide_keys.1 = (f32[8,128,512]{2,1,0:T(8,128)S(1)}, f32[8,8,512]{2,1,0:T(8,128)S(1)}) custom-call(bf16[512,1024]{1,0:T(8,128)(2,1)S(1)} %bitcast.45, f32[8,128,512]{2,1,0:T(8,128)S(1)} %copy-done.6, f32[8,8,512]{2,1,0:T(8,128)S(1)} %get-tuple-element.12.sum_in, bf16[32,2,32,128]{3,2,1,0:T(8,128)(2,1)S(1)} %collective-permute-done.10.refs_0_.refs_12_), custom_call_target="tpu_custom_call" | custom-call | flops 4294967296 | bytes 6291456 | tf_op jit(solution)/shard_map/wide_keys/pallas_call | solution.py:324
  48.5 0.0 collective-permute-done.13.refs_5_.refs_14_
  48.5 0.6 collective-permute-done.14.refs_4_
  49.1 0.0 collective-permute-start.15
  49.1 0.7 collective-permute-start.17
  49.9 0.0 collective-permute-done.16.refs_0_.refs_13_
  49.9 5.2 %wide_keys_s.1 = (f32[8,128,512]{2,1,0:T(8,128)S(1)}, f32[8,8,512]{2,1,0:T(8,128)S(1)}) custom-call(bf16[512,1024]{1,0:T(8,128)(2,1)S(1)} %bitcast.46, f32[8,128,512]{2,1,0:T(8,128)S(1)} %get-tuple-element.18.acc_in, f32[8,8,512]{2,1,0:T(8,128)S(1)} %get-tuple-element.16.sum_in, bf16[32,2,32,128]{3,2,1,0:T(8,128)(2,1)} %collective-permute-done.16.refs_0_.refs_13_), custom_call_target="tpu_custom_call" | custom-call | flops 4294967296 | bytes 6291456 | tf_op jit(solution)/shard_map/wide_keys_s/pallas_call | solution.py:324
  55.1 0.0 collective-permute-done.17.refs_6_.refs_15_
  55.1 0.0 copy-start.1
  55.1 70.1 %last_keys.1 = bf16[512,1024]{1,0:T(8,128)(2,1)} custom-call(s32[1,8]{1,0:T(1,128)S(1)} %copy-done.4, s32[1]{0:T(128)S(6)} %copy.10.len_ref.refs_1_, bf16[512,1024]{1,0:T(8,128)(2,1)S(1)} %bitcast.47, f32[8,128,512]{2,1,0:T(8,128)S(1)} %get-tuple-element.19.refs_3_, f32[8,8,512]{2,1,0:T(8,128)S(1)} %get-tuple-element.20.refs_4_, ...), custom_call_target="tpu_custom_call" | custom-call | flops 4294967296 | bytes 6291456 | tf_op jit(solution)/shard_map/last_keys/pallas_call | solution.py:344
  125.2 0.0 collective-permute-done.15.refs_5_
  125.2 0.0 collective-permute-done.12.refs_3_
  125.2 0.0 copy-done.1
  125.2 42.0 %prompt_rows.1 = bf16[512,512]{1,0:T(8,128)(2,1)} custom-call(s32[4]{0:T(128)S(1)} %pad_add_fusion.place_ref, bf16[512,512]{1,0:T(8,128)(2,1)S(1)} %copy-done.1, bf16[16,2,32,128]{3,2,1,0:T(8,128)(2,1)S(1)} %get-tuple-element.23.refs_0_, bf16[16,2,32,128]{3,2,1,0:T(8,128)(2,1)S(1)} %get-tuple-element.25.refs_1_, ...), custom_call_target="tpu_custom_call" | custom-call | flops 8589934592 | bytes 6291456 | tf_op jit(solution)/shard_map/prompt_rows/pallas_call | solution.py:370
  (11 shorter events, 0.3 us)
Async XLA Ops:
  1.7 6.3 %collective-permute-start = (bf16[2,32,256]{2,1,0:T(8,128)(2,1)S(1)}, bf16[2,32,256]{2,1,0:T(8,128)(2,1)S(1)}, u32[]{:S(2)}, u32[]{:S(2)}) collective-permute-start(bf16[2,32,256]{2,1,0:T(8,128)(2,1)S(1)} %get-tuple-element.35), channel_id=1, source_target_pairs={{0,32},{1,33},{4,36},{5,37},{8,40},{9,41},{12,44},{13,45},{2,34},{... | collective-permute-start | bytes 98312 | tf_op jit(solution)/shard_map/ppermute | solution.py:32
  1.7 6.8 %collective-permute-start.1 = (bf16[2,32,256]{2,1,0:T(8,128)(2,1)S(1)}, bf16[2,32,256]{2,1,0:T(8,128)(2,1)S(1)}, u32[]{:S(2)}, u32[]{:S(2)}) collective-permute-start(bf16[2,32,256]{2,1,0:T(8,128)(2,1)S(1)} %get-tuple-element.36), channel_id=1, source_target_pairs={{0,96},{1,97},{4,100},{5,101},{8,104},{9,105},{12,108},{13,109},{2... | collective-permute-start | bytes 98312 | tf_op jit(solution)/shard_map/ppermute | solution.py:32
  3.2 5.3 %collective-permute-start.2 = (bf16[2,32,256]{2,1,0:T(8,128)(2,1)S(1)}, bf16[2,32,256]{2,1,0:T(8,128)(2,1)S(1)}, u32[]{:S(2)}, u32[]{:S(2)}) collective-permute-start(bf16[2,32,256]{2,1,0:T(8,128)(2,1)S(1)} %get-tuple-element.37), channel_id=1, source_target_pairs={{0,64},{1,65},{4,68},{5,69},{8,72},{9,73},{12,76},{13,77},{2,66},{... | collective-permute-start | bytes 98312 | tf_op jit(solution)/shard_map/ppermute | solution.py:32
  4.9 3.6 %collective-permute-start.4 = (bf16[2,32,256]{2,1,0:T(8,128)(2,1)S(1)}, bf16[2,32,256]{2,1,0:T(8,128)(2,1)S(1)}, u32[]{:S(2)}, u32[]{:S(2)}) collective-permute-start(bf16[2,32,256]{2,1,0:T(8,128)(2,1)S(1)} %get-tuple-element.40), channel_id=1, source_target_pairs={{0,12},{1,13},{4,0},{5,1},{8,4},{9,5},{12,8},{13,9},{2,14},{3,15},... | collective-permute-start | bytes 98312 | tf_op jit(solution)/shard_map/ppermute | solution.py:32
  7.4 4.3 %collective-permute-start.5 = (bf16[2,32,256]{2,1,0:T(8,128)(2,1)S(1)}, bf16[2,32,256]{2,1,0:T(8,128)(2,1)S(1)}, u32[]{:S(2)}, u32[]{:S(2)}) collective-permute-start(bf16[2,32,256]{2,1,0:T(8,128)(2,1)S(1)} %get-tuple-element.41), channel_id=1, source_target_pairs={{0,8},{1,9},{4,12},{5,13},{8,0},{9,1},{12,4},{13,5},{2,10},{3,11},... | collective-permute-start | bytes 98312 | tf_op jit(solution)/shard_map/ppermute | solution.py:32
  7.9 4.1 %collective-permute-start.3 = (bf16[2,32,256]{2,1,0:T(8,128)(2,1)S(1)}, bf16[2,32,256]{2,1,0:T(8,128)(2,1)S(1)}, u32[]{:S(2)}, u32[]{:S(2)}) collective-permute-start(bf16[2,32,256]{2,1,0:T(8,128)(2,1)S(1)} %get-tuple-element.39), channel_id=1, source_target_pairs={{0,4},{1,5},{4,8},{5,9},{8,12},{9,13},{12,0},{13,1},{2,6},{3,7},{6... | collective-permute-start | bytes 98312 | tf_op jit(solution)/shard_map/ppermute | solution.py:32
  12.2 6.2 %collective-permute-start.6 = (bf16[2,4,2,32,128]{4,3,2,1,0:T(8,128)(2,1)S(1)}, bf16[2,4,2,32,128]{4,3,2,1,0:T(8,128)(2,1)S(1)}, u32[]{:S(2)}, u32[]{:S(2)}) collective-permute-start(bf16[2,4,2,32,128]{4,3,2,1,0:T(8,128)(2,1)S(1)} %pad_maximum_fusion.5), channel_id=1, source_target_pairs={{0,2},{1,3},{4,6},{5,7},{8,10},{9,11},{12,14},{13,15},{2,16},{3,17... | collective-permute-start | bytes 393224 | tf_op jit(solution)/shard_map/ppermute | solution.py:32
  13.9 4.5 %collective-permute-start.7 = (bf16[2,4,2,32,128]{4,3,2,1,0:T(8,128)(2,1)S(1)}, bf16[2,4,2,32,128]{4,3,2,1,0:T(8,128)(2,1)S(1)}, u32[]{:S(2)}, u32[]{:S(2)}) collective-permute-start(bf16[2,4,2,32,128]{4,3,2,1,0:T(8,128)(2,1)S(1)} %pad_maximum_fusion.6), channel_id=1, source_target_pairs={{0,18},{1,19},{4,22},{5,23},{8,26},{9,27},{12,30},{13,31},{2,0},{3... | collective-permute-start | bytes 393224 | tf_op jit(solution)/shard_map/ppermute | solution.py:32
  16.1 5.5 %collective-permute-start.8 = (bf16[2,4,2,32,128]{4,3,2,1,0:T(8,128)(2,1)S(1)}, bf16[2,4,2,32,128]{4,3,2,1,0:T(8,128)(2,1)S(1)}, u32[]{:S(2)}, u32[]{:S(2)}) collective-permute-start(bf16[2,4,2,32,128]{4,3,2,1,0:T(8,128)(2,1)S(1)} %pad_maximum_fusion.7), channel_id=1, source_target_pairs={{0,16},{1,17},{4,20},{5,21},{8,24},{9,25},{12,28},{13,29},{2,18},{... | collective-permute-start | bytes 393224 | tf_op jit(solution)/shard_map/ppermute | solution.py:32
  21.7 6.0 %collective-permute-start.9 = (bf16[2,16,2,32,128]{4,3,2,1,0:T(8,128)(2,1)S(1)}, bf16[2,16,2,32,128]{4,3,2,1,0:T(8,128)(2,1)S(1)}, u32[]{:S(2)}, u32[]{:S(2)}) collective-permute-start(bf16[2,16,2,32,128]{4,3,2,1,0:T(8,128)(2,1)S(1)} %pad_maximum_fusion), channel_id=1, source_target_pairs={{0,1},{1,0},{4,5},{5,4},{8,9},{9,8},{12,13},{13,12},{2,3},{3,2},{6... | collective-permute-start | bytes 1572872 | tf_op jit(solution)/shard_map/ppermute | solution.py:32
  26.9 2.1 %copy-start = (bf16[1,512,1024]{2,1,0:T(8,128)(2,1)S(1)}, bf16[1,512,1024]{2,1,0:T(8,128)(2,1)}, u32[]{:S(2)}) copy-start(bf16[1,512,1024]{2,1,0:T(8,128)(2,1)} %param.11) | copy-start | bytes 3145732
  26.9 2.1 %copy-start.2 = (bf16[1,512,128]{2,1,0:T(8,128)(2,1)S(1)}, bf16[1,512,128]{2,1,0:T(8,128)(2,1)}, u32[]{:S(2)}) copy-start(bf16[1,512,128]{2,1,0:T(8,128)(2,1)} %param.12) | copy-start | bytes 393220
  26.9 2.1 %copy-start.3 = (bf16[1,512,128]{2,1,0:T(8,128)(2,1)S(1)}, bf16[1,512,128]{2,1,0:T(8,128)(2,1)}, u32[]{:S(2)}) copy-start(bf16[1,512,128]{2,1,0:T(8,128)(2,1)} %param.13) | copy-start | bytes 393220
  26.9 2.0 %copy-start.4 = (s32[1,8]{1,0:T(1,128)S(1)}, s32[1,8]{1,0:T(1,128)}, u32[]{:S(2)}) copy-start(s32[1,8]{1,0:T(1,128)} %refs_0_.1) | copy-start | bytes 100
  27.9 9.9 %collective-permute-start.10 = (bf16[32,2,32,128]{3,2,1,0:T(8,128)(2,1)S(1)}, bf16[32,2,32,128]{3,2,1,0:T(8,128)(2,1)S(1)}, u32[]{:S(2)}, u32[]{:S(2)}) collective-permute-start(bf16[32,2,32,128]{3,2,1,0:T(8,128)(2,1)S(1)} %pad_maximum_fusion.1), channel_id=1, source_target_pairs={{0,4},{1,13},{4,8},{5,1},{8,12},{9,5},{12,0},{13,9},{2,6},{3,15},{... | collective-permute-start | bytes 1572872 | tf_op jit(solution)/shard_map/ppermute | solution.py:32
  28.1 9.7 %collective-permute-start.11 = (bf16[32,2,32,128]{3,2,1,0:T(8,128)(2,1)S(1)}, bf16[32,2,32,128]{3,2,1,0:T(8,128)(2,1)S(1)}, u32[]{:S(2)}, u32[]{:S(2)}) collective-permute-start(bf16[32,2,32,128]{3,2,1,0:T(8,128)(2,1)S(1)} %pad_maximum_fusion.2), channel_id=1, source_target_pairs={{0,32},{1,97},{4,36},{5,101},{8,40},{9,105},{12,44},{13,109},{2,34... | collective-permute-start | bytes 1572872 | tf_op jit(solution)/shard_map/ppermute | solution.py:32
  36.4 1.4 copy-start.5
  37.8 12.1 %collective-permute-start.16 = (bf16[32,2,32,128]{3,2,1,0:T(8,128)(2,1)S(1)}, bf16[32,2,32,128]{3,2,1,0:T(8,128)(2,1)}, u32[]{:S(2)}, u32[]{:S(2)}) collective-permute-start(bf16[32,2,32,128]{3,2,1,0:T(8,128)(2,1)S(1)} %collective-permute-done.10.refs_0_.refs_12_), channel_id=1, source_target_pairs={{0,1},{1,0},{4,5},{5,4},{8,9},{9,8},{12,13},{13,12},{2,3},{3,2},{6... | collective-permute-start | bytes 1572872 | tf_op jit(solution)/shard_map/ppermute | solution.py:32
  39.6 85.6 %collective-permute-start.12 = (bf16[32,2,32,128]{3,2,1,0:T(8,128)(2,1)S(1)}, bf16[32,2,32,128]{3,2,1,0:T(8,128)(2,1)S(1)}, u32[]{:S(2)}, u32[]{:S(2)}) collective-permute-start(bf16[32,2,32,128]{3,2,1,0:T(8,128)(2,1)S(1)} %collective-permute-done.11.refs_2_), channel_id=1, source_target_pairs={{0,1},{1,0},{4,5},{5,4},{8,9},{9,8},{12,13},{13,12},{2,3},{3,2},{6... | collective-permute-start | bytes 1572872 | tf_op jit(solution)/shard_map/ppermute | solution.py:32
  39.7 8.8 %collective-permute-start.13 = (bf16[16,2,32,128]{3,2,1,0:T(8,128)(2,1)S(1)}, bf16[16,2,32,128]{3,2,1,0:T(8,128)(2,1)S(1)}, u32[]{:S(2)}, u32[]{:S(2)}) collective-permute-start(bf16[16,2,32,128]{3,2,1,0:T(8,128)(2,1)S(1)} %slice.22), channel_id=1, source_target_pairs={{0,4},{1,13},{4,8},{5,1},{8,12},{9,5},{12,0},{13,9},{2,6},{3,15},{... | collective-permute-start | bytes 786440 | tf_op jit(solution)/shard_map/ppermute | solution.py:32
  42.7 6.4 %collective-permute-start.14 = (bf16[16,2,32,128]{3,2,1,0:T(8,128)(2,1)S(1)}, bf16[16,2,32,128]{3,2,1,0:T(8,128)(2,1)S(1)}, u32[]{:S(2)}, u32[]{:S(2)}) collective-permute-start(bf16[16,2,32,128]{3,2,1,0:T(8,128)(2,1)S(1)} %slice.23), channel_id=1, source_target_pairs={{0,32},{1,97},{4,36},{5,101},{8,40},{9,105},{12,44},{13,109},{2,34... | collective-permute-start | bytes 786440 | tf_op jit(solution)/shard_map/ppermute | solution.py:32
  42.7 1.6 copy-start.6
  49.1 76.0 %collective-permute-start.15 = (bf16[16,2,32,128]{3,2,1,0:T(8,128)(2,1)S(1)}, bf16[16,2,32,128]{3,2,1,0:T(8,128)(2,1)S(1)}, u32[]{:S(2)}, u32[]{:S(2)}) collective-permute-start(bf16[16,2,32,128]{3,2,1,0:T(8,128)(2,1)S(1)} %collective-permute-done.14.refs_4_), channel_id=1, source_target_pairs={{0,1},{1,0},{4,5},{5,4},{8,9},{9,8},{12,13},{13,12},{2,3},{3,2},{6... | collective-permute-start | bytes 786440 | tf_op jit(solution)/shard_map/ppermute | solution.py:32
  49.1 6.0 %collective-permute-start.17 = (bf16[16,2,32,128]{3,2,1,0:T(8,128)(2,1)S(1)}, bf16[16,2,32,128]{3,2,1,0:T(8,128)(2,1)S(1)}, u32[]{:S(2)}, u32[]{:S(2)}) collective-permute-start(bf16[16,2,32,128]{3,2,1,0:T(8,128)(2,1)S(1)} %collective-permute-done.13.refs_5_.refs_14_), channel_id=1, source_target_pairs={{0,1},{1,0},{4,5},{5,4},{8,9},{9,8},{12,13},{13,12},{2,3},{3,2},{6... | collective-permute-start | bytes 786440 | tf_op jit(solution)/shard_map/ppermute | solution.py:32
  55.1 70.1 %copy-start.1 = (bf16[512,512]{1,0:T(8,128)(2,1)S(1)}, bf16[512,512]{1,0:T(8,128)(2,1)}, u32[]{:S(2)}) copy-start(bf16[512,512]{1,0:T(8,128)(2,1)} %q_ref.1) | copy-start | bytes 1572868
